TPU v7x, 128 devices: a whole 4x4x4 slice. The times are simulated.
128 devices in a mesh: ccd: 32 (over z, x, core), visit: 4 (over y).
Axes of the slice: x: 4, y: 4, z: 4, core: 2. Of those that a mesh axis runs over, the one named last changes fastest.
Arguments:
- image: bfloat16 [4, 32, 2048, 1024], P('visit', 'ccd'), may hold values from -6 to 6
- coefs: float32 [4, 32, 3], P('visit', 'ccd'), may hold values from -3 to 3
- basis_width: float32 [3], replicated, may hold values from 0.7 to 3
- psf_width: float32 [1], replicated, may hold values from 1.3 to 2.8
- warp_rows: bfloat16 [4, 32, 2048, 2048], P('visit', 'ccd'), may hold values from -1 to 2
- warp_cols: bfloat16 [4, 32, 1024, 1024], P('visit', 'ccd'), may hold values from -1 to 2
- visit_weight: int32 [4], P('visit'), may hold values from 1 to 4
- dest_patch: int32 [4, 32, 32, 1], P('visit', 'ccd'), may hold values from 0 to 31; in each aligned block of 32 rows (0 to 31, 32 to 63, ..., all dimensions but the last counted through in order) at most 2 rows name the same one
- dest_slot: int32 [4, 32, 32], P('visit', 'ccd'), may hold values from 0 to 31
Outputs:
- coadd_map: float32 [65536, 1024], P('ccd', 'visit')
- detection: float32 [65536, 1024], P('ccd', 'visit')
Inputs may be any that keep to these rules, and one draw needn't show every extreme that they name: `dest_patch`: in the 32 rows of one device no patch is named more than 2 times, and in every draw some patch is named exactly 2 times by some device.
All inputs are finite; a program needn't handle non-finite values.
Results may differ from a plain program's by a relative error of at most 0.0075.
Values may be sent and summed in bfloat16 or wider, within the bound.
A program may use at most 128 MiB of HBM per device.

v0:
```python
import jax
import jax.numpy as jnp
from jax import lax
from jax.sharding import PartitionSpec as P

NBASIS = 3
HALF = 10


floor_level = 0.05


def extended(value, sides, width):
    for axis, dim in sides:
        size, length = (lax.axis_size(axis), value.shape[dim])
        up = [(i, (i + 1) % size) for i in range(size - 1)]
        down = [(j, i) for i, j in up]
        last = lax.slice_in_dim(value, length - width, length, axis=dim)
        leading = lax.slice_in_dim(value, 0, width, axis=dim)
        before = lax.ppermute(last, axis, up)
        after = lax.ppermute(leading, axis, down)
        value = jnp.concatenate([before, value, after], axis=dim)
    return value


def gauss_taps(sigma_px, half_span):
    offsets = (jnp.arange(2 * half_span + 1) - half_span).astype(jnp.float32)
    values = jnp.exp(-offsets * offsets / (2.0 * sigma_px * sigma_px))
    return values / jnp.sum(values)


def band_table(tap_row, block_len, extent):
    tap_count = tap_row.shape[0]
    row_ids = lax.broadcasted_iota(jnp.int32, (block_len, block_len + extent), 0)
    col_ids = lax.broadcasted_iota(jnp.int32, (block_len, block_len + extent), 1)
    offset = col_ids - row_ids
    matches = offset[:, :, None] == jnp.arange(tap_count, dtype=jnp.int32)[None, None, :]
    return jnp.sum(jnp.where(matches, tap_row.astype(jnp.float32)[None, None, :], 0.0), axis=2)


def windows(padded, block_len, extent, axis_num):
    block_count = (padded.shape[axis_num] - extent) // block_len
    slices_list = [
        lax.slice_in_dim(
            padded, number * block_len, number * block_len + block_len + extent, axis=axis_num
        )
        for number in range(block_count)
    ]
    return jnp.stack(slices_list, axis=axis_num)


def round_up(amount, stride_len):
    return -(-amount // stride_len) * stride_len


def smooth_rows(padded, band_mat, block_len, extent, precision):
    stacked = windows(padded, block_len, extent, 0)
    result = jnp.einsum(
        "ij,kjc->kic", band_mat, stacked, preferred_element_type=jnp.float32, precision=precision
    )
    return result.reshape((-1,) + padded.shape[1:])


def smooth_cols(padded, band_mat, block_len, extent, precision):
    stacked = windows(padded, block_len, extent, 1)
    result = jnp.einsum(
        "rkj,ij->rki", stacked, band_mat, preferred_element_type=jnp.float32, precision=precision
    )
    return result.reshape(padded.shape[0], -1)


def place_visit(inbox_rows, inbox_slots, blocks, weight, rows_here, cols_here):
    placing = (
        inbox_slots.reshape(1, -1).astype(jnp.float32)
        == jnp.arange(blocks, dtype=jnp.float32)[:, None]
    ).astype(jnp.bfloat16)
    summed = jnp.dot(
        placing, inbox_rows.reshape(-1, inbox_rows.shape[-1]), preferred_element_type=jnp.float32
    )
    partial_value = (weight * summed).astype(jnp.bfloat16).reshape(rows_here, cols_here)
    return lax.optimization_barrier(partial_value).astype(jnp.float32)


def local(
    image, coefs, basis_width, psf_width, warp_rows, warp_cols, visit_weight, dest_patch, dest_slot
):
    rows_here = image.shape[2]
    cols_here = image.shape[3]
    ccd_count = lax.axis_size("ccd")
    visit_count = lax.axis_size("visit")
    blocks = dest_slot.shape[2]
    piece_rows = rows_here // blocks
    capacity = max(2, 2 * blocks // ccd_count)
    ccd_index = lax.axis_index("ccd")
    visit_index = lax.axis_index("visit")
    row_block = min(128, rows_here)
    col_block = min(128, cols_here)
    row_extent = round_up(2 * HALF, 8)
    col_extent = round_up(2 * HALF, col_block)
    highest = lax.Precision.HIGHEST
    pixels = image[0, 0]
    mixing = coefs[0, 0]
    tap_sets = [
        lax.optimization_barrier(gauss_taps(basis_width[number], HALF).astype(jnp.bfloat16))
        for number in range(NBASIS)
    ]
    padded = jnp.pad(pixels, ((HALF, row_extent - HALF), (0, 0)))
    stacked = windows(padded, row_block, row_extent, 0)
    row_bands = jnp.stack(
        [band_table(tap_row, row_block, row_extent) for tap_row in tap_sets]
    ).astype(jnp.bfloat16)
    rowpass = jnp.einsum("bij,kjc->bkic", row_bands, stacked, preferred_element_type=jnp.float32)
    rowpass = rowpass.reshape(NBASIS, rows_here, cols_here).astype(jnp.bfloat16)
    matched = jnp.zeros((rows_here, cols_here), jnp.float32)
    for number in range(NBASIS):
        col_band = band_table(tap_sets[number], col_block, col_extent).astype(jnp.bfloat16)
        widened = jnp.pad(rowpass[number], ((0, 0), (HALF, col_extent - HALF)))
        matched = matched + mixing[number] * smooth_cols(
            widened, col_band, col_block, col_extent, None
        )
    matched = matched.astype(jnp.bfloat16)
    halfway = jnp.dot(warp_rows[0, 0], matched, preferred_element_type=jnp.float32).astype(
        jnp.bfloat16
    )
    warped = jnp.dot(halfway, warp_cols[0, 0], preferred_element_type=jnp.float32).astype(
        jnp.bfloat16
    )
    chosen = dest_patch.reshape(-1)
    slot_ids = dest_slot.reshape(-1)
    earlier = lax.broadcasted_iota(jnp.int32, (blocks, blocks), 1) < lax.broadcasted_iota(
        jnp.int32, (blocks, blocks), 0
    )
    rank_in = jnp.sum((chosen[:, None] == chosen[None, :]) & earlier, axis=1)
    target = chosen * capacity + rank_in
    routing = jnp.arange(ccd_count * capacity, dtype=jnp.int32)[:, None] == target[None, :]
    outbox_slots = (jnp.sum(jnp.where(routing, slot_ids[None, :] + 1, 0), axis=1) - 1).astype(
        jnp.bfloat16
    )
    weight = visit_weight[0].astype(jnp.float32)
    part_cols = cols_here // visit_count
    cells_here = chosen * blocks + slot_ids
    cell_count = ccd_count * blocks
    hit_table = jnp.arange(cell_count, dtype=jnp.int32)[:, None] == cells_here[None, :]
    coverage = lax.psum(jnp.sum(jnp.where(hit_table, weight, 0.0), axis=1), ("ccd", "visit"))
    cover_rows = jnp.broadcast_to(coverage[:, None], (cell_count, piece_rows)).reshape(-1)
    cover_pad = jnp.pad(cover_rows, (HALF, HALF))
    segment = lax.dynamic_slice_in_dim(cover_pad, ccd_index * rows_here, rows_here + 2 * HALF)
    own_cover = segment[HALF : HALF + rows_here]
    psf_taps = gauss_taps(psf_width[0], HALF)
    squared = psf_taps * psf_taps
    col_pos = visit_index * part_cols - HALF + jnp.arange(part_cols + 2 * HALF, dtype=jnp.int32)
    inside = ((col_pos >= 0) & (col_pos < cols_here)).astype(jnp.float32)
    depth_rows = jnp.zeros((rows_here,), jnp.float32)
    depth_cols = jnp.zeros((part_cols,), jnp.float32)
    for number in range(2 * HALF + 1):
        depth_rows = depth_rows + squared[number] * segment[number : number + rows_here]
        depth_cols = depth_cols + squared[number] * inside[number : number + part_cols]
    outbox = jnp.dot(
        routing.astype(jnp.bfloat16),
        warped.reshape(blocks, piece_rows * cols_here),
        preferred_element_type=jnp.float32,
    ).astype(jnp.bfloat16)
    inbox_rows, inbox_slots = (
        lax.all_to_all(
            outbox.reshape(ccd_count, capacity, piece_rows * cols_here),
            "ccd",
            split_axis=0,
            concat_axis=0,
            tiled=True,
        ),
        lax.all_to_all(
            outbox_slots.reshape(ccd_count, capacity),
            "ccd",
            split_axis=0,
            concat_axis=0,
            tiled=True,
        ),
    )
    visit_term = place_visit(inbox_rows, inbox_slots, blocks, weight, rows_here, cols_here)
    total_full = lax.psum(visit_term.astype(jnp.bfloat16), "visit").astype(jnp.float32)
    row_framed = extended(total_full.astype(jnp.bfloat16), (("ccd", 0),), HALF).astype(
        total_full.dtype
    )
    widened_full = jnp.pad(row_framed, ((0, 0), (HALF, HALF)))
    framed = lax.dynamic_slice_in_dim(
        widened_full, visit_index * part_cols, part_cols + 2 * HALF, 1
    )
    total_here = lax.dynamic_slice_in_dim(total_full, visit_index * part_cols, part_cols, 1)
    det_block = min(128, part_cols)
    det_extent = round_up(2 * HALF, det_block)
    psf_rows = band_table(psf_taps, row_block, row_extent)
    psf_cols = band_table(psf_taps, det_block, det_extent)
    framed = jnp.pad(framed, ((0, row_extent - 2 * HALF), (0, det_extent - 2 * HALF)))
    across = smooth_rows(framed, psf_rows, row_block, row_extent, highest)
    signal = smooth_cols(across, psf_cols, det_block, det_extent, highest)
    coadd_map = total_here / jnp.maximum(own_cover, 1.0)[:, None]
    detection = signal / jnp.sqrt(
        jnp.maximum(depth_rows[:, None] * depth_cols[None, :], floor_level)
    )
    return (coadd_map, detection)


def solution(mesh):
    placed = (
        P("visit", "ccd", None, None),
        P("visit", "ccd", None),
        P(),
        P(),
        P("visit", "ccd", None, None),
        P("visit", "ccd", None, None),
        P("visit"),
        P("visit", "ccd", None, None),
        P("visit", "ccd", None),
    )
    return jax.shard_map(
        local,
        mesh=mesh,
        in_specs=placed,
        out_specs=(P("ccd", "visit"), P("ccd", "visit")),
        check_vma=False,
    )
```

profile of v0, /device:TPU:7, one launch (start us, length us, event | category | flops | bytes accessed | tf_op | source)
XLA Modules:
  0.0 421.4 jit_solution(11949149709678435215)
XLA Ops:
  9.7 8.7 %all-to-all-start = ((bf16[32,1,2]{2,1,0:T(2,128)(2,1)}), bf16[32,1,2]{2,1,0:T(2,128)(2,1)S(1)}, u32[]{:S(2)}, u32[]{:S(2)}) async-start(bf16[32,1,2]{2,1,0:T(2,128)(2,1)} %convert_element_type.159), calls=%async_computation | async-start | bytes 32768 | tf_op jit(solution)/shard_map/all_to_all | solution.py:171
  22.0 2.2 copy-done.3
  35.3 11.1 %convert_bitcast_fusion = bf16[3,16,128,1024]{3,2,0,1:T(8,128)(2,1)} fusion(bf16[16,152,1024]{2,1,0:T(8,128)(2,1)} %copy-done.3, bf16[1,128,152]{1,2,0:T(8,128)(2,1)S(1)} %bitcast.325, bf16[1,128,152]{1,2,0:T(8,128)(2,1)S(1)} %bitcast.326, bf16[1,128,152]{1,2,0:T(8,128)(2,1)S(1)} %bitcast.327), kind=kOutput, calls=%fused_computation.3 | convolution fusion | flops 1919244288 | bytes 17680384 | tf_op jit(solution)/shard_map/bij,kjc->bkic/dot_general | solution.py:112
  46.4 5.9 %fusion.113 = (bf16[1,16,128,1024]{3,2,0,1:T(8,128)(2,1)S(1)}, bf16[1,16,128,1024]{3,2,0,1:T(8,128)(2,1)S(1)}, bf16[1,16,128,1024]{3,2,0,1:T(8,128)(2,1)S(1)}) fusion(bf16[3,16,128,1024]{3,2,0,1:T(8,128)(2,1)} %convert_bitcast_fusion), kind=kLoop, calls=%fused_computation.237 | loop fusion | bytes 25165824 | tf_op jit(solution)/shard_map/slice | solution.py:117
  61.4 1.9 copy-done.4
  66.2 3.1 copy-done.5
  69.2 3.0 fusion.89
  72.3 6.0 %fusion.91 = f32[2048,8,128]{0,2,1:T(8,128)} fusion(bf16[2048,8,256]{2,0,1:T(8,128)(2,1)S(1)} %bitcast.322, bf16[128,256]{1,0:T(8,128)(2,1)S(1)} %get-tuple-element.5), kind=kOutput, calls=%fused_computation.169 | convolution fusion | flops 1073741824 | bytes 16842752 | tf_op jit(solution)/shard_map/rkj,ij->rki/dot_general | solution.py:66
  78.3 12.1 %add_convert_fusion = bf16[2048,8,128]{0,2,1:T(8,128)(2,1)S(1)} fusion(f32[2048,8,128]{0,2,1:T(8,128)S(1)} %fusion.89, f32[2048,8,128]{0,2,1:T(8,128)} %fusion.91, bf16[2048,8,256]{2,0,1:T(8,128)(2,1)} %copy-done.5, f32[]{:T(128)} %bitcast.52, f32[]{:T(128)} %bitcast.41, f32[]{:T(128)} %bitcast.3, bf16[128,256]{1,0:T(8,128)(2,1)S(1)} %get-tuple-element.3), kind=kOutput, calls=%fused_computation.6 | convolution fusion | flops 1086324736 | bytes 29425676 | tf_op jit(solution)/shard_map/rkj,ij->rki/dot_general | solution.py:66
  90.5 11.5 %fusion.1 = bf16[1024,2048]{1,0:T(8,128)(2,1)S(1)} fusion(bf16[2048,1024]{0,1:T(8,128)(2,1)S(1)} %bitcast.323, bf16[1,1,2048,2048]{3,2,1,0:T(8,128)(2,1)} %param.13), kind=kOutput, calls=%fused_computation.4 | convolution fusion | flops 8589934592 | bytes 16777216 | tf_op jit(solution)/shard_map/dot_general | solution.py:122
  102.0 6.1 %fusion.10 = bf16[2048,1024]{1,0:T(8,128)(2,1)} fusion(bf16[1024,2048]{1,0:T(8,128)(2,1)S(1)} %fusion.1, bf16[1,1,1024,1024]{3,2,1,0:T(8,128)(2,1)S(1)} %copy-done), kind=kOutput, calls=%fused_computation.21 | convolution fusion | flops 4297064448 | bytes 10485760 | tf_op jit(solution)/shard_map/dot_general | solution.py:125
  108.1 6.0 %reshape.166 = bf16[32,65536]{1,0:T(8,128)(2,1)} reshape(bf16[2048,1024]{1,0:T(8,128)(2,1)} %fusion.10) | data formatting | bytes 8388608 | tf_op jit(solution)/shard_map/reshape | solution.py:160
  114.1 7.9 %convolution_convert_fusion = bf16[64,65536]{1,0:T(8,128)(2,1)} fusion(bf16[32,65536]{1,0:T(8,128)(2,1)} %reshape.166, s32[32]{0:T(128)S(1)} %get-tuple-element.41), kind=kOutput, calls=%fused_computation | convolution fusion | flops 272631808 | bytes 12583040 | tf_op jit(solution)/shard_map/dot_general | solution.py:158
  122.0 10.6 %reshape.167 = bf16[32,2,65536]{2,1,0:T(2,128)(2,1)} reshape(bf16[64,65536]{1,0:T(8,128)(2,1)} %convolution_convert_fusion) | data formatting | bytes 16777216 | tf_op jit(solution)/shard_map/reshape | solution.py:165
  132.5 7.4 %all-to-all-start.1 = ((bf16[32,2,65536]{2,1,0:T(2,128)(2,1)}), bf16[32,2,65536]{2,1,0:T(2,128)(2,1)}, u32[]{:S(2)}, u32[]{:S(2)}) async-start(bf16[32,2,65536]{2,1,0:T(2,128)(2,1)} %reshape.167), calls=%async_computation.1 | async-start | bytes 16777216 | tf_op jit(solution)/shard_map/all_to_all | solution.py:164
  140.8 100.6 %all-to-all-done.1 = bf16[32,2,65536]{2,1,0:T(2,128)(2,1)} async-done(((bf16[32,2,65536]{2,1,0:T(2,128)(2,1)}), bf16[32,2,65536]{2,1,0:T(2,128)(2,1)}, u32[]{:S(2)}, u32[]{:S(2)}) %all-to-all-start.1) | async-done | bytes 8388640 | tf_op jit(solution)/shard_map/all_to_all | solution.py:164
  241.4 10.2 %reshape.168 = bf16[64,65536]{1,0:T(8,128)(2,1)} reshape(bf16[32,2,65536]{2,1,0:T(2,128)(2,1)} %all-to-all-done.1) | data formatting | bytes 16777216 | tf_op jit(solution)/shard_map/reshape | solution.py:78
  251.6 6.6 %fusion = bf16[32,65536]{1,0:T(8,128)(2,1)} fusion(bf16[64,65536]{1,0:T(8,128)(2,1)} %reshape.168, f32[]{:T(128)} %bitcast, f32[64]{0:T(128)S(1)} %reshape.173), kind=kOutput, calls=%fused_computation.2 | convolution fusion | flops 272631808 | bytes 12583172 | tf_op jit(solution)/shard_map/dot_general | solution.py:77
  258.2 5.6 %reshape.169 = bf16[2048,1024]{1,0:T(8,128)(2,1)} reshape(bf16[32,65536]{1,0:T(8,128)(2,1)} %fusion) | data formatting | bytes 8388608 | tf_op jit(solution)/shard_map/reshape | solution.py:80
  264.0 68.7 %psum.15 = f32[1024]{0:T(1024)S(1)} all-reduce(f32[1024]{0:T(1024)S(1)} %select_reduce_fusion.8), channel_id=1, replica_groups=mesh['ccd'=32,'visit'=4] {'ccd','visit'}, use_global_device_ids=true, to_apply=%region_13.14 | all-reduce | flops 1024 | bytes 8192 | tf_op jit(solution)/shard_map/psum | solution.py:144
  334.4 13.4 %fusion.97 = f32[2048]{0:T(1024)S(1)} fusion(s32[]{:T(128)S(6)} %add.274, s32[]{:T(128)S(6)} %add.273, s32[]{:T(128)S(6)} %add.272, f32[65536]{0:T(1024)S(1)} %reshape.170, s32[]{:T(128)S(6)} %select_n.52, s32[]{:T(128)S(6)} %add.256, s32[]{:T(128)S(6)} %add.257, s32[]{:T(128)S(6)} %add.258, s32[]{:T(128)S(6)} %add.259, s32[]{:T(128)S(6)} %add.260, ...), kind=kLoop, calls=%fused_computation.185 | loop fusion | flops 83968 | bytes 270504 | tf_op jit(solution)/shard_map/add | solution.py:156
  347.9 13.2 %multiply_add_fusion = f32[256]{0:T(256)S(1)} fusion(f32[276]{0:T(512)S(1)} %fusion.105, f32[]{:T(128)} %bitcast.111, f32[]{:T(128)} %bitcast.110, f32[]{:T(128)} %bitcast.109, f32[]{:T(128)} %bitcast.108, f32[]{:T(128)} %bitcast.107, f32[]{:T(128)} %bitcast.106, f32[]{:T(128)} %bitcast.105, f32[]{:T(128)} %bitcast.104, f32[]{:T(128)} %bitcast.103, ...), kind=kLoop, calls=%fused_computation.216 | loop fusion | flops 10496 | bytes 22612 | tf_op jit(solution)/shard_map/add | solution.py:157
  361.9 3.6 collective-permute-start
  365.5 1.9 collective-permute-start.1
  367.4 2.9 convert_divide_fusion
  370.3 2.5 collective-permute-done.1
  372.8 23.0 %concatenate.3 = bf16[2068,1024]{1,0:T(8,128)(2,1)} concatenate(bf16[10,1024]{1,0:T(8,128)(2,1)S(1)} %collective-permute-done, bf16[2048,1024]{1,0:T(8,128)(2,1)} %all-reduce.9.cloned.1.call-done, bf16[10,1024]{1,0:T(8,128)(2,1)S(1)} %collective-permute-done.1), dimensions={0} | concatenate | bytes 8470528 | tf_op jit(solution)/shard_map/concatenate | solution.py:22
  395.9 2.5 fusion.14
  398.8 3.1 fusion.86
  402.2 5.8 %fusion.4 = f32[2048,2,128]{0,2,1:T(8,128)} fusion(f32[2048,1,256]{2,0,1:T(8,128)S(1)} %get-tuple-element.18, f32[2048,1,256]{2,0,1:T(8,128)S(1)} %get-tuple-element.17, f32[128,256]{1,0:T(8,128)S(1)} %get-tuple-element.2), kind=kOutput, calls=%fused_computation.15 | convolution fusion | flops 1611661312 | bytes 6422528 | tf_op jit(solution)/shard_map/rkj,ij->rki/dot_general | solution.py:66
  408.0 3.1 copy.16
  411.1 3.3 rsqrt_multiply_fusion
  (112 shorter events, 27.8 us)
Async XLA Ops:
  7.2 94.8 %copy-start = (bf16[1,1,1024,1024]{3,2,1,0:T(8,128)(2,1)S(1)}, bf16[1,1,1024,1024]{3,2,1,0:T(8,128)(2,1)}, u32[]{:S(2)}) copy-start(bf16[1,1,1024,1024]{3,2,1,0:T(8,128)(2,1)} %param.14) | copy-start | bytes 6291460
  9.7 122.8 %all-to-all-start = ((bf16[32,1,2]{2,1,0:T(2,128)(2,1)}), bf16[32,1,2]{2,1,0:T(2,128)(2,1)S(1)}, u32[]{:S(2)}, u32[]{:S(2)}) async-start(bf16[32,1,2]{2,1,0:T(2,128)(2,1)} %convert_element_type.159), calls=%async_computation | async-start | bytes 32768 | tf_op jit(solution)/shard_map/all_to_all | solution.py:171
  18.4 2.3 copy-start.2
  21.4 4.7 %copy-start.6 = (f32[3]{0:T(128)S(1)}, f32[3]{0:T(128)}, u32[]{:S(2)}) copy-start(f32[3]{0:T(128)} %param.11) | copy-start | bytes 40
  22.0 2.2 copy-start.3
  60.1 3.2 copy-start.4
  64.6 0.9 copy-start.7
  65.0 7.2 %slice-start = ((s8[8388608]{0:T(1024)(128)(4,1)}), s8[4194304]{0:T(1024)(128)(4,1)S(1)}, s32[]{:S(2)}) async-start(s8[8388608]{0:T(1024)(128)(4,1)} %bitcast.321), calls=%async_computation.3 | async-start | bytes 8388608
  65.5 3.7 copy-start.5
  69.2 3.0 slice-start.1
  132.5 108.9 %all-to-all-start.1 = ((bf16[32,2,65536]{2,1,0:T(2,128)(2,1)}), bf16[32,2,65536]{2,1,0:T(2,128)(2,1)}, u32[]{:S(2)}, u32[]{:S(2)}) async-start(bf16[32,2,65536]{2,1,0:T(2,128)(2,1)} %reshape.167), calls=%async_computation.1 | async-start | bytes 16777216 | tf_op jit(solution)/shard_map/all_to_all | solution.py:164
  140.0 221.1 %all-reduce.9.cloned.1.call-start = ((), (), s32[]{:S(2)}) async-start(), calls=%async_computation.2 | async-start | bytes 8388608 | tf_op jit(solution)/shard_map/psum | solution.py:180
  361.9 8.4 %collective-permute-start = (bf16[10,1024]{1,0:T(8,128)(2,1)S(1)}, bf16[10,1024]{1,0:T(8,128)(2,1)S(1)}, u32[]{:S(2)}, u32[]{:S(2)}) collective-permute-start(bf16[10,1024]{1,0:T(8,128)(2,1)S(1)} %get-tuple-element.16), channel_id=1, source_target_pairs={{0,4},{4,8},{8,12},{12,16},{16,20},{20,24},{24,28},{28,32},{32,36}... | collective-permute-start | bytes 61448 | tf_op jit(solution)/shard_map/ppermute | solution.py:20
  365.5 7.3 %collective-permute-start.1 = (bf16[10,1024]{1,0:T(8,128)(2,1)S(1)}, bf16[10,1024]{1,0:T(8,128)(2,1)S(1)}, u32[]{:S(2)}, u32[]{:S(2)}) collective-permute-start(bf16[10,1024]{1,0:T(8,128)(2,1)S(1)} %get-tuple-element.15), channel_id=1, source_target_pairs={{4,0},{8,4},{12,8},{16,12},{20,16},{24,20},{28,24},{32,28},{36,32}... | collective-permute-start | bytes 61448 | tf_op jit(solution)/shard_map/ppermute | solution.py:21
  408.0 6.4 %copy-start.1 = (bf16[1,1,1024,1024]{3,2,1,0:T(8,128)(2,1)S(1)}, bf16[1,1,1024,1024]{3,2,1,0:T(8,128)(2,1)}, u32[]{:S(2)}) copy-start(bf16[1,1,1024,1024]{3,2,1,0:T(8,128)(2,1)} %param.14) | copy-start | bytes 6291460
Sparse Core Ops, SparseCore 0:
  264.0 95.0 all-reduce.8
where the time goes:
time: 430 us; the launch traced here: 421 us
  waiting for transfers between devices  103 us (24%)
  local copies, waits for them, and re-layouts  90.4 us (21%)
  matrix products  73.3 us (17%)
  blocking collectives  68.7 us (16%)
  other arithmetic  44.2 us (10%)
  starting transfers between devices  21.7 us (5%)
  between operations  20 us (5%)
    all_to_all x1, waiting for transfers between devices, local(): lax.all_to_all(outbox.reshape(ccd_count, capacity, piece_rows * cols_here...  101 us
    psum x1, blocking collectives, local(): lax.psum(jnp.sum(jnp.where(hit_table, weight, 0.0), axis=1), ('ccd', 'vis...  68.7 us
    dot_general x4, matrix products, smooth_cols(): jnp.einsum('rkj,ij->rki', stacked, band_mat, preferred_element_type=jnp.f...  27 us
    concatenate x1, local copies, waits for them, and re-layouts, extended(): value = jnp.concatenate([before, value, after], axis=dim)  23 us
    unnamed x71, local copies, waits for them, and re-layouts  19.6 us
    add x1, other arithmetic, local(): depth_rows + squared[number] * segment[number:number + rows_here]  13.4 us
    add x1, other arithmetic, local(): depth_cols + squared[number] * inside[number:number + part_cols]  13.2 us
    dot_general x1, matrix products, local(): jnp.dot(warp_rows[0, 0], matched, preferred_element_type=jnp.float32)  11.5 us
  transfers between devices with their start and end apart: 5, of which 2 were waited for; matrix products, arithmetic and copies ran while one was open for 31% of the time, Pallas kernels for 0%

commit v1 on v0

v1 whole, which is shorter than its diff:
```python
import functools

import jax
import jax.numpy as jnp
from jax import lax
from jax.experimental import pallas as pl
from jax.experimental.pallas import tpu as pltpu
from jax.sharding import PartitionSpec as P

NBASIS = 3
HALF = 10
ROWS = 2048
COLS = 1024
BLOCKS = 32
PIECE = 64
VISITS = 4
CCDS = 32
DEVICES = VISITS * CCDS
CELLS = CCDS * BLOCKS
PIECES = DEVICES * BLOCKS
PART = COLS // VISITS
WIDE = 2 * PART
FLOOR = 0.05
VMEM_LIMIT = 60 * 1024 * 1024

F32 = jnp.float32
BF16 = jnp.bfloat16


def dot(a, b):
    return jnp.dot(a, b, preferred_element_type=F32)


def gauss_norm(two_var):
    m = lax.broadcasted_iota(jnp.int32, (1, 128), 1)
    d = (m - HALF).astype(F32)
    return jnp.sum(jnp.where(m <= 2 * HALF, jnp.exp(-d * d / two_var), 0.0), axis=1, keepdims=True)


def gauss_at(d, two_var, norm):
    df = d.astype(F32)
    return jnp.where(jnp.abs(d) <= HALF, jnp.exp(-df * df / two_var) / norm, 0.0)


def warp_kernel(coefs, widths, image, warp_rows, warp_cols, out, img, rp, matched, wr, wc, wf, rb, cb, sems):
    copies = [
        pltpu.make_async_copy(image.at[pl.ds(512 * n, 512)], img.at[pl.ds(16 + 512 * n, 512)], sems.at[n])
        for n in range(4)
    ]
    wr_copies = [
        pltpu.make_async_copy(warp_rows.at[pl.ds(512 * n, 512)], wr.at[pl.ds(512 * n, 512)], sems.at[4 + n])
        for n in range(4)
    ]
    wc_copy = pltpu.make_async_copy(warp_cols, wc, sems.at[8])
    for c in copies:
        c.start()
    for c in wr_copies[:1] + [wc_copy] + wr_copies[1:]:
        c.start()
    img[0:16, :] = jnp.zeros((16, COLS), BF16)
    img[ROWS + 16 : ROWS + 32, :] = jnp.zeros((16, COLS), BF16)
    rp[:, :, 0:128] = jnp.zeros((NBASIS, ROWS, 128), BF16)
    rp[:, :, COLS + 128 : COLS + 256] = jnp.zeros((NBASIS, ROWS, 128), BF16)
    d_row = lax.broadcasted_iota(jnp.int32, (128, 160), 1) - 16 - lax.broadcasted_iota(jnp.int32, (128, 160), 0)
    d_col = lax.broadcasted_iota(jnp.int32, (512, 256), 0) - 128 - lax.broadcasted_iota(jnp.int32, (512, 256), 1)
    for b in range(NBASIS):
        sigma = widths[b]
        two_var = 2.0 * sigma * sigma
        norm = gauss_norm(two_var)
        rb[b * 128 : (b + 1) * 128, :] = gauss_at(d_row, two_var, norm).astype(BF16)
        cb[b] = gauss_at(d_col, two_var, norm).astype(BF16)

    def row_block(n, carry):
        y = pl.multiple_of(n * 128, 128)
        res = dot(rb[...], img[pl.ds(y, 160), :]).astype(BF16)
        for b in range(NBASIS):
            rp[b, pl.ds(y, 128), 128 : COLS + 128] = res[b * 128 : (b + 1) * 128]
        return carry

    for c in copies:
        c.wait()
    lax.fori_loop(0, ROWS // 128, row_block, 0)

    def col_block(n, carry):
        y = pl.multiple_of(n * 512, 512)
        for q in range(VISITS):
            acc = coefs[0] * dot(rp[0, pl.ds(y, 512), q * 256 : q * 256 + 512], cb[0])
            for b in range(1, NBASIS):
                acc = acc + coefs[b] * dot(rp[b, pl.ds(y, 512), q * 256 : q * 256 + 512], cb[b])
            matched[pl.ds(y, 512), q * 256 : (q + 1) * 256] = acc.astype(BF16)
        return carry

    lax.fori_loop(0, ROWS // 512, col_block, 0)
    wc_copy.wait()
    for c in wr_copies:
        c.wait()

    def warp_block(n, carry):
        y = pl.multiple_of(n * 256, 256)
        halfway = dot(wr[pl.ds(y, 256), :], matched[...]).astype(BF16)
        warped = dot(halfway, wc[...])
        for l in range(COLS // 128):
            wf[l, pl.ds(y, 256), :] = warped[:, l * 128 : (l + 1) * 128]
        return carry

    for g in range(2):
        lax.fori_loop(4 * g, 4 * g + 4, warp_block, 0)

        def pack(c, carry):
            for i in range(2):
                for l in range(COLS // 128):
                    rows = wf[l, pl.ds(g * 1024 + c + 32 * i, 16, stride=PIECE), :]
                    j, h = divmod(l, 2)
                    out[c * VISITS + j, g * 16 : (g + 1) * 16, i * 256 + h * 128 : i * 256 + (h + 1) * 128] = rows.astype(BF16)
            return carry

        lax.fori_loop(0, CCDS, pack, 0)


def warp_window(coefs, widths, image, warp_rows, warp_cols):
    smem = pl.BlockSpec(memory_space=pltpu.SMEM)
    hbm = pl.BlockSpec(memory_space=pl.ANY)
    return pl.pallas_call(
        warp_kernel,
        out_shape=jax.ShapeDtypeStruct((DEVICES, BLOCKS, WIDE), BF16),
        in_specs=[smem, smem, hbm, hbm, hbm],
        out_specs=pl.BlockSpec(memory_space=pltpu.VMEM),
        scratch_shapes=[
            pltpu.VMEM((ROWS + 32, COLS), BF16),
            pltpu.VMEM((NBASIS, ROWS, COLS + 256), BF16),
            pltpu.VMEM((ROWS, COLS), BF16),
            pltpu.VMEM((ROWS, ROWS), BF16),
            pltpu.VMEM((COLS, COLS), BF16),
            pltpu.VMEM((COLS // 128, ROWS, 128), F32),
            pltpu.VMEM((NBASIS * 128, 160), BF16),
            pltpu.VMEM((NBASIS, 512, 256), BF16),
            pltpu.SemaphoreType.DMA((9,)),
        ],
        compiler_params=pltpu.CompilerParams(vmem_limit_bytes=VMEM_LIMIT),
        cost_estimate=pl.CostEstimate(flops=22_000_000_000, bytes_accessed=18 << 20, transcendentals=0),
        name="warp_window",
    )(coefs, widths, image, warp_rows, warp_cols)


def cell_sum_kernel(cells, weights, inbox, out, acc):
    n = pl.program_id(0)
    step = cells.shape[1]
    ids = lax.broadcasted_iota(jnp.int32, (CELLS, step), 0)
    placing = jnp.where(ids == cells[...], weights[...], 0.0).astype(BF16)
    part = dot(placing, inbox[...])

    @pl.when(n == 0)
    def _():
        acc[...] = part

    @pl.when(n > 0)
    def _():
        acc[...] += part

    @pl.when(n == pl.num_programs(0) - 1)
    def _():
        out[...] = acc[...].astype(BF16)


def cell_sum(cells, weights, inbox):
    step = 512
    return pl.pallas_call(
        cell_sum_kernel,
        out_shape=jax.ShapeDtypeStruct((CELLS, WIDE), BF16),
        grid=(PIECES // step,),
        in_specs=[
            pl.BlockSpec((1, step), lambda n: (0, n)),
            pl.BlockSpec((1, step), lambda n: (0, n)),
            pl.BlockSpec((step, WIDE), lambda n: (n, 0)),
        ],
        out_specs=pl.BlockSpec((CELLS, WIDE), lambda n: (0, 0)),
        scratch_shapes=[pltpu.VMEM((CELLS, WIDE), F32)],
        compiler_params=pltpu.CompilerParams(vmem_limit_bytes=VMEM_LIMIT),
        name="cell_sum",
    )(cells, weights, inbox)


def order_kernel(inbox, total, edges, buf):
    for h in range(WIDE // 128):
        for c in range(CCDS):
            buf[h, c * BLOCKS : (c + 1) * BLOCKS, :] = inbox[c, :, h * 128 : (h + 1) * 128].astype(F32)

    for s in range(BLOCKS):
        for h in range(WIDE // 128):
            i, l = divmod(h, 2)
            rows = buf[h, pl.ds(s, CCDS, stride=BLOCKS), :]
            total[s * PIECE + i * 32 : s * PIECE + (i + 1) * 32, l * 128 : (l + 1) * 128] = rows.astype(BF16)
    e = lax.broadcasted_iota(jnp.int32, (32, PART), 0)
    x = lax.broadcasted_iota(jnp.int32, (32, PART), 1)
    pick = (x == jnp.where(e < 16, e, e + PART - 32)).astype(F32).astype(BF16)
    edges[...] = lax.dot_general(pick, total[...], (((1,), (1,)), ((), ())), preferred_element_type=F32).astype(BF16)


def order_rows(inbox):
    return pl.pallas_call(
        order_kernel,
        out_shape=(jax.ShapeDtypeStruct((ROWS, PART), BF16), jax.ShapeDtypeStruct((32, ROWS), BF16)),
        scratch_shapes=[pltpu.VMEM((WIDE // 128, CCDS * BLOCKS, 128), F32)],
        compiler_params=pltpu.CompilerParams(vmem_limit_bytes=VMEM_LIMIT),
        name="order_rows",
    )(inbox)


def split_bf16(v):
    hi = v.astype(BF16)
    return hi, (v - hi.astype(F32)).astype(BF16)


def detect_kernel(place, width, cover, total, above, below, edges, coadd, detection, ext):
    column0 = place[0] * PART
    ext[0:16, 0:PART] = above[...]
    ext[16 : ROWS + 16, 0:PART] = total[...]
    ext[ROWS + 16 : ROWS + 32, 0:PART] = below[...]
    e = lax.broadcasted_iota(jnp.int32, (32, 128), 0)
    x = lax.broadcasted_iota(jnp.int32, (32, 128), 1)
    pick = (e == x).astype(F32).astype(BF16)
    ext[:, PART : PART + 128] = lax.dot_general(
        edges[...], pick, (((0,), (0,)), ((), ())), preferred_element_type=F32
    )[0 : ROWS + 32].astype(BF16)
    sigma = width[0]
    two_var = 2.0 * sigma * sigma
    norm = gauss_norm(two_var)
    d_row = lax.broadcasted_iota(jnp.int32, (128, 160), 1) - 16 - lax.broadcasted_iota(jnp.int32, (128, 160), 0)
    row_hi, row_lo = split_bf16(gauss_at(d_row, two_var, norm))
    k = lax.broadcasted_iota(jnp.int32, (PART + 128, PART), 0)
    x = lax.broadcasted_iota(jnp.int32, (PART + 128, PART), 1)
    source = jnp.where(k < PART, k, jnp.where(k < PART + 16, k - PART - 16, jnp.where(k < PART + 32, k - 16, 4 * COLS)))
    col_hi, col_lo = split_bf16(gauss_at(source - x, two_var, norm))

    xs = lax.broadcasted_iota(jnp.int32, (1, PART), 1) + column0
    zero = jnp.zeros((1, PART), F32)
    depth_cols = zero
    r = lax.broadcasted_iota(jnp.int32, (PIECE, PART), 0)
    here = jnp.zeros((PIECE, PART), F32)
    before = jnp.zeros((PIECE, PART), F32)
    after = jnp.zeros((PIECE, PART), F32)
    for m in range(2 * HALF + 1):
        d = float(m - HALF)
        tap = jnp.exp(jnp.full((1, PART), -d * d, F32) / two_var) / norm
        sq = tap * tap
        at = xs + (m - HALF)
        depth_cols = depth_cols + jnp.where((at >= 0) & (at < COLS), sq, 0.0)
        row = r + (m - HALF)
        before = before + jnp.where(row < 0, sq, 0.0)
        after = after + jnp.where(row >= PIECE, sq, 0.0)
        here = here + jnp.where((row >= 0) & (row < PIECE), sq, 0.0)

    def block(n, carry):
        y = pl.multiple_of(n * 128, 128)
        window = ext[pl.ds(y, 160), :]
        across = dot(row_hi, window) + dot(row_lo, window)
        a_hi, a_lo = split_bf16(across)
        signal = dot(a_hi, col_hi) + (dot(a_lo, col_hi) + dot(a_hi, col_lo))
        for h in range(2):
            s = n * 2 + h
            c = cover[s + 1]
            depth_rows = cover[s] * before + c * here + cover[s + 2] * after
            scale = lax.rsqrt(jnp.maximum(depth_rows * depth_cols, FLOOR))
            rows = pl.ds(pl.multiple_of(y + h * PIECE, PIECE), PIECE)
            detection[rows, :] = signal[h * PIECE : (h + 1) * PIECE] * scale
            own = ext[pl.ds(pl.multiple_of(y + h * PIECE + 16, 16), PIECE), 0:PART].astype(F32)
            coadd[rows, :] = own / jnp.maximum(jnp.full((PIECE, PART), c, F32), 1.0)
        return carry

    lax.fori_loop(0, ROWS // 128, block, 0)


def detect(place, width, cover, total, above, below, edges):
    smem = pl.BlockSpec(memory_space=pltpu.SMEM)
    vmem = pl.BlockSpec(memory_space=pltpu.VMEM)
    out = jax.ShapeDtypeStruct((ROWS, PART), F32)
    return pl.pallas_call(
        detect_kernel,
        out_shape=(out, out),
        in_specs=[smem, smem, smem, vmem, vmem, vmem, vmem],
        scratch_shapes=[pltpu.VMEM((ROWS + 32, PART + 128), BF16)],
        compiler_params=pltpu.CompilerParams(vmem_limit_bytes=VMEM_LIMIT),
        name="detect",
    )(place, width, cover, total, above, below, edges)


def local(image, coefs, basis_width, psf_width, warp_rows, warp_cols, visit_weight, dest_patch, dest_slot):
    ccd = lax.axis_index("ccd")
    visit = lax.axis_index("visit")
    cells = dest_patch.reshape(-1) * BLOCKS + dest_slot.reshape(-1)
    tagged = lax.all_gather(cells * 8 + visit_weight[0], ("ccd", "visit"), tiled=True)
    outbox = warp_window(coefs.reshape(-1), basis_width, image[0, 0], warp_rows[0, 0], warp_cols[0, 0])
    inbox = lax.all_to_all(outbox, ("ccd", "visit"), split_axis=0, concat_axis=0, tiled=True)
    all_cells = (tagged // 8).reshape(1, PIECES)
    weights = (tagged % 8).astype(F32).reshape(1, PIECES)
    summed = cell_sum(all_cells, weights, inbox.reshape(PIECES, WIDE))
    near = ccd * BLOCKS - 1 + jnp.arange(BLOCKS + 2, dtype=jnp.int32)
    cover = jnp.sum(jnp.where(all_cells == near[:, None], weights, 0.0), axis=1)
    rows_in = lax.all_to_all(summed.reshape(CCDS, BLOCKS, WIDE), "ccd", split_axis=0, concat_axis=0, tiled=True)
    total, edges = order_rows(rows_in)
    up = [(n, n + 1) for n in range(CCDS - 1)]
    down = [(n + 1, n) for n in range(CCDS - 1)]
    right = [(n, n + 1) for n in range(VISITS - 1)]
    left = [(n + 1, n) for n in range(VISITS - 1)]
    above = lax.ppermute(total[ROWS - 16 :], "ccd", up)
    below = lax.ppermute(total[:16], "ccd", down)
    edges_above = jnp.concatenate([above[:, :16], above[:, PART - 16 :]], axis=1).T
    edges_below = jnp.concatenate([below[:, :16], below[:, PART - 16 :]], axis=1).T
    pad = jnp.zeros((32, 96), BF16)
    edges = jnp.concatenate([edges_above, edges, edges_below, pad], axis=1)
    from_left = lax.ppermute(edges[16:], "visit", right)
    from_right = lax.ppermute(edges[:16], "visit", left)
    edges = jnp.concatenate([from_left, from_right], axis=0)
    return detect(visit[None], psf_width, cover, total, above, below, edges)


def solution(mesh):
    placed = (
        P("visit", "ccd", None, None),
        P("visit", "ccd", None),
        P(),
        P(),
        P("visit", "ccd", None, None),
        P("visit", "ccd", None, None),
        P("visit"),
        P("visit", "ccd", None, None),
        P("visit", "ccd", None),
    )
    return jax.shard_map(
        local,
        mesh=mesh,
        in_specs=placed,
        out_specs=(P("ccd", "visit"), P("ccd", "visit")),
        check_vma=False,
    )
```

time: 430 us -> 231 us (0.54)
  the two profiles are of different devices: /device:TPU:7 before, /device:TPU:1 now
where the time goes in v1:
time: 231 us; the launch traced here: 226 us
  blocking collectives  103 us (45%)
  Pallas kernels  67 us (29%)
  starting transfers between devices  27 us (12%)
  waiting for transfers between devices  20.2 us (9%)
  local copies, waits for them, and re-layouts  4.39 us (2%)
    unnamed x1, blocking collectives  103 us
    pallas_call x1, Pallas kernels, warp_window(): pl.pallas_call(warp_kernel, out_shape=jax.ShapeDtypeStruct((DEVICES, BLOC...  41.2 us
    all_to_all x1, waiting for transfers between devices, local(): lax.all_to_all(summed.reshape(CCDS, BLOCKS, WIDE), 'ccd', split_axis=0, c...  17.2 us
    pallas_call x1, Pallas kernels, detect(): pl.pallas_call(detect_kernel, out_shape=(out, out), in_specs=[smem, smem,...  12.2 us
    all_to_all x1, starting transfers between devices, local(): lax.all_to_all(outbox, ('ccd', 'visit'), split_axis=0, concat_axis=0, til...  12 us
    pallas_call x1, Pallas kernels, cell_sum(): pl.pallas_call(cell_sum_kernel, out_shape=jax.ShapeDtypeStruct((CELLS, WI...  9.78 us
    all_to_all x1, starting transfers between devices, local(): lax.all_to_all(summed.reshape(CCDS, BLOCKS, WIDE), 'ccd', split_axis=0, c...  5.97 us
  transfers between devices with their start and end apart: 6, of which 3 were waited for; matrix products, arithmetic and copies ran while one was open for 1% of the time, Pallas kernels for 0%

profile of v1, /device:TPU:1, one launch (start us, length us, event | category | flops | bytes accessed | tf_op | source)
XLA Modules:
  0.0 226.3 jit_solution(6638698411539225539)
XLA Ops:
  0.6 41.2 %warp_window.1 = bf16[128,32,512]{2,1,0:T(8,128)(2,1)} custom-call(f32[3]{0:T(128)} %bitcast.31, f32[3]{0:T(128)} %widths.1, bf16[2048,1024]{1,0:T(8,128)(2,1)} %bitcast.29, bf16[2048,2048]{1,0:T(8,128)(2,1)} %bitcast.28, bf16[1024,1024]{1,0:T(8,128)(2,1)} %bitcast.30), custom_call_target="tpu_custom_call" | custom-call | flops 22000001024 | bytes 18874368 | tf_op jit(solution)/shard_map/warp_window/pallas_call | solution.py:122
  41.8 0.0 copy-start.3
  41.8 0.0 copy-start.4
  41.8 12.0 %all-to-all-start = ((bf16[128,32,512]{2,1,0:T(8,128)(2,1)}), bf16[128,32,512]{2,1,0:T(8,128)(2,1)}, u32[]{:S(2)}, u32[]{:S(2)}) async-start(bf16[128,32,512]{2,1,0:T(8,128)(2,1)} %warp_window.1), calls=%async_computation | async-start | bytes 8388608 | tf_op jit(solution)/shard_map/all_to_all | solution.py:292
  54.5 0.0 copy-done.3
  54.5 0.0 copy-done.4
  54.5 0.1 fusion.5
  54.6 103.3 %all-reduce = s32[4096]{0:T(1024)S(1)} all-reduce(s32[4096]{0:T(1024)S(1)} %fusion.5), channel_id=1, replica_groups=mesh['ccd'=32,'visit'=4] {'ccd','visit'}, use_global_device_ids=true, to_apply=%add | all-reduce | flops 4096 | bytes 32768
  158.0 0.6 add_select_fusion.1
  158.6 0.0 all-to-all-done
  158.6 9.8 %cell_sum.1 = bf16[1024,512]{1,0:T(8,128)(2,1)} custom-call(s32[1,4096]{1,0:T(1,128)} %bitcast.26, f32[1,4096]{1,0:T(1,128)} %bitcast.27, bf16[4096,512]{1,0:T(8,128)(2,1)} %bitcast.10.inbox), custom_call_target="tpu_custom_call" | custom-call | tf_op jit(solution)/shard_map/cell_sum/pallas_call | solution.py:166
  168.4 6.0 %all-to-all-start.1 = ((bf16[32,32,512]{2,1,0:T(8,128)(2,1)}), bf16[32,32,512]{2,1,0:T(8,128)(2,1)S(1)}, u32[]{:S(2)}, u32[]{:S(2)}) async-start(bf16[32,32,512]{2,1,0:T(8,128)(2,1)} %bitcast.25), calls=%async_computation.1 | async-start | bytes 2097152 | tf_op jit(solution)/shard_map/all_to_all | solution.py:298
  174.4 17.2 %all-to-all-done.1.inbox = bf16[32,32,512]{2,1,0:T(8,128)(2,1)S(1)} async-done(((bf16[32,32,512]{2,1,0:T(8,128)(2,1)}), bf16[32,32,512]{2,1,0:T(8,128)(2,1)S(1)}, u32[]{:S(2)}, u32[]{:S(2)}) %all-to-all-start.1) | async-done | bytes 1048608 | tf_op jit(solution)/shard_map/all_to_all | solution.py:298
  191.5 1.0 copy-done
  192.5 3.9 %order_rows.1 = (bf16[2048,256]{1,0:T(8,128)(2,1)}, bf16[32,2048]{1,0:T(8,128)(2,1)}) custom-call(bf16[32,32,512]{2,1,0:T(8,128)(2,1)} %copy-done), custom_call_target="tpu_custom_call" | custom-call | tf_op jit(solution)/shard_map/order_rows/pallas_call | solution.py:199
  196.4 0.7 fusion.6
  197.1 0.1 copy.16
  197.2 2.3 %collective-permute-start.1 = (bf16[16,256]{0,1:T(8,128)(2,1)S(1)}, bf16[16,256]{0,1:T(8,128)(2,1)S(1)}, u32[]{:S(2)}, u32[]{:S(2)}) collective-permute-start(bf16[16,256]{0,1:T(8,128)(2,1)S(1)} %copy.16), channel_id=1, source_target_pairs={{4,0},{8,4},{12,8},{16,12},{20,16},{24,20},{28,24},{32,28},{36,32}... | collective-permute-start | bytes 24584 | tf_op jit(solution)/shard_map/ppermute | solution.py:305
  200.2 0.1 copy.15
  200.3 3.3 %collective-permute-start = (bf16[16,256]{0,1:T(8,128)(2,1)S(1)}, bf16[16,256]{0,1:T(8,128)(2,1)S(1)}, u32[]{:S(2)}, u32[]{:S(2)}) collective-permute-start(bf16[16,256]{0,1:T(8,128)(2,1)S(1)} %copy.15), channel_id=1, source_target_pairs={{0,4},{4,8},{8,12},{12,16},{16,20},{20,24},{24,28},{28,32},{32,36}... | collective-permute-start | bytes 24584 | tf_op jit(solution)/shard_map/ppermute | solution.py:304
  203.6 0.0 collective-permute-done.1
  203.6 1.3 collective-permute-done
  204.9 1.1 concatenate.14
  206.0 2.2 collective-permute-start.2
  208.2 1.3 collective-permute-start.3
  209.5 0.8 select_reduce_fusion.cover
  210.3 0.7 copy.17.above
  211.0 0.7 copy.18.below
  211.7 0.0 collective-permute-done.2
  211.7 1.8 collective-permute-done.3
  213.5 0.7 pad_maximum_fusion.edges
  214.1 12.2 %detect.1 = (f32[2048,256]{1,0:T(8,128)}, f32[2048,256]{1,0:T(8,128)}) custom-call(s32[1]{0:T(128)} %bitcast.place, f32[1]{0:T(128)S(6)} %copy.20.width, f32[34]{0:T(128)} %select_reduce_fusion.cover, bf16[2048,256]{1,0:T(8,128)(2,1)} %get-tuple-element.4.total, bf16[16,256]{1,0:T(8,128)(2,1)} %copy.17.above, bf16[16,256]{1,0:T(8,128)(2,1)} %copy.18.below, ...), custom_call_target="tpu_custom_call" | custom-call | tf_op jit(solution)/shard_map/detect/pallas_call | solution.py:276
  (12 shorter events, 0.0 us)
Async XLA Ops:
  41.8 12.7 %copy-start.3 = (s32[1,1,32]{2,1,0:T(1,128)S(1)}, s32[1,1,32]{2,1,0:T(1,128)}, u32[]{:S(2)}) copy-start(s32[1,1,32]{2,1,0:T(1,128)} %param.17) | copy-start | bytes 388
  41.8 12.7 %copy-start.4 = (s32[1,1,32,1]{2,3,1,0:T(1,128)S(1)}, s32[1,1,32,1]{2,3,1,0:T(1,128)}, u32[]{:S(2)}) copy-start(s32[1,1,32,1]{2,3,1,0:T(1,128)} %param.16) | copy-start | bytes 388
  41.8 116.8 %all-to-all-start = ((bf16[128,32,512]{2,1,0:T(8,128)(2,1)}), bf16[128,32,512]{2,1,0:T(8,128)(2,1)}, u32[]{:S(2)}, u32[]{:S(2)}) async-start(bf16[128,32,512]{2,1,0:T(8,128)(2,1)} %warp_window.1), calls=%async_computation | async-start | bytes 8388608 | tf_op jit(solution)/shard_map/all_to_all | solution.py:292
  158.6 50.9 %copy-start.1 = (s32[4096]{0:T(1024)S(1)}, s32[4096]{0:T(1024)}, u32[]{:S(2)}) copy-start(s32[4096]{0:T(1024)} %get-tuple-element.14) | copy-start | bytes 49156
  158.6 50.9 %copy-start.2 = (f32[4096]{0:T(1024)S(1)}, f32[4096]{0:T(1024)}, u32[]{:S(2)}) copy-start(f32[4096]{0:T(1024)} %get-tuple-element.15) | copy-start | bytes 49156
  168.4 23.2 %all-to-all-start.1 = ((bf16[32,32,512]{2,1,0:T(8,128)(2,1)}), bf16[32,32,512]{2,1,0:T(8,128)(2,1)S(1)}, u32[]{:S(2)}, u32[]{:S(2)}) async-start(bf16[32,32,512]{2,1,0:T(8,128)(2,1)} %bitcast.25), calls=%async_computation.1 | async-start | bytes 2097152 | tf_op jit(solution)/shard_map/all_to_all | solution.py:298
  191.5 1.0 copy-start
  197.2 6.4 %collective-permute-start.1 = (bf16[16,256]{0,1:T(8,128)(2,1)S(1)}, bf16[16,256]{0,1:T(8,128)(2,1)S(1)}, u32[]{:S(2)}, u32[]{:S(2)}) collective-permute-start(bf16[16,256]{0,1:T(8,128)(2,1)S(1)} %copy.16), channel_id=1, source_target_pairs={{4,0},{8,4},{12,8},{16,12},{20,16},{24,20},{28,24},{32,28},{36,32}... | collective-permute-start | bytes 24584 | tf_op jit(solution)/shard_map/ppermute | solution.py:305
  200.3 4.6 %collective-permute-start = (bf16[16,256]{0,1:T(8,128)(2,1)S(1)}, bf16[16,256]{0,1:T(8,128)(2,1)S(1)}, u32[]{:S(2)}, u32[]{:S(2)}) collective-permute-start(bf16[16,256]{0,1:T(8,128)(2,1)S(1)} %copy.15), channel_id=1, source_target_pairs={{0,4},{4,8},{8,12},{12,16},{16,20},{20,24},{24,28},{28,32},{32,36}... | collective-permute-start | bytes 24584 | tf_op jit(solution)/shard_map/ppermute | solution.py:304
  206.0 5.7 %collective-permute-start.2 = (bf16[16,2176]{1,0:T(8,128)(2,1)S(1)}, bf16[16,2176]{1,0:T(8,128)(2,1)S(1)}, u32[]{:S(2)}, u32[]{:S(2)}) collective-permute-start(bf16[16,2176]{1,0:T(8,128)(2,1)S(1)} %get-tuple-element.8), channel_id=1, source_target_pairs={{0,1},{1,2},{2,3},{4,5},{5,6},{6,7},{8,9},{9,10},{10,11},{12,13},{... | collective-permute-start | bytes 208904 | tf_op jit(solution)/shard_map/ppermute | solution.py:310
  208.2 5.3 %collective-permute-start.3 = (bf16[16,2176]{1,0:T(8,128)(2,1)S(1)}, bf16[16,2176]{1,0:T(8,128)(2,1)S(1)}, u32[]{:S(2)}, u32[]{:S(2)}) collective-permute-start(bf16[16,2176]{1,0:T(8,128)(2,1)S(1)} %get-tuple-element.9), channel_id=1, source_target_pairs={{1,0},{2,1},{3,2},{5,4},{6,5},{7,6},{9,8},{10,9},{11,10},{13,12},{... | collective-permute-start | bytes 208904 | tf_op jit(solution)/shard_map/ppermute | solution.py:311

commit v2 on v1

v2 whole, which is shorter than its diff:
```python
import functools

import jax
import jax.numpy as jnp
from jax import lax
from jax.experimental import pallas as pl
from jax.experimental.pallas import tpu as pltpu
from jax.sharding import PartitionSpec as P

NBASIS = 3
HALF = 10
ROWS = 2048
COLS = 1024
BLOCKS = 32
PIECE = 64
VISITS = 4
CCDS = 32
DEVICES = VISITS * CCDS
CELLS = CCDS * BLOCKS
PIECES = DEVICES * BLOCKS
PART = COLS // VISITS
WIDE = 2 * PART
FLOOR = 0.05
MESH = pl.DeviceIdType.MESH
STRIDE = PIECE + 1
GROUP = 16
GROUPS = BLOCKS // GROUP
CHUNK = 512
TAIL = ROWS + 256
VMEM_LIMIT = 60 * 1024 * 1024

F32 = jnp.float32
BF16 = jnp.bfloat16


def dot(a, b):
    return jnp.dot(a, b, preferred_element_type=F32)


def gauss_norm(two_var):
    m = lax.broadcasted_iota(jnp.int32, (1, 128), 1)
    d = (m - HALF).astype(F32)
    return jnp.sum(jnp.where(m <= 2 * HALF, jnp.exp(-d * d / two_var), 0.0), axis=1, keepdims=True)


def gauss_at(d, two_var, norm):
    df = d.astype(F32)
    return jnp.where(jnp.abs(d) <= HALF, jnp.exp(-df * df / two_var) / norm, 0.0)


def shifted(steps):
    ccd, y = lax.axis_index("ccd"), lax.axis_index("visit")
    z, x, core = ccd // 8, lax.rem(ccd // 2, 4), lax.rem(ccd, 2)
    z = lax.rem(z + steps // 32, 4)
    x = lax.rem(x + lax.rem(steps // 8, 4), 4)
    core = lax.rem(core + lax.rem(steps // 4, 2), 2)
    y = lax.rem(y + lax.rem(steps, 4), 4)
    return z * 8 + x * 2 + core, y


def partner(k):
    return shifted(lax.rem(k * 59, DEVICES))


def patch_partner(k):
    return shifted(4 * lax.rem(k * 11, CCDS))


def coadd_kernel(
    coefs, widths, tags, image, warp_rows, warp_cols, ext, cover,
    img, rp, matched, wr, wc, wf, rb, cb, outbox, inbox, tags_in, acc, sumbox, rows_in, ordered, edges, turned, above, below,
    local_sems, tag_send, tag_recv, out_send, out_recv, sum_send, sum_recv, halo_send, halo_recv,
):
    ccd, visit = lax.axis_index("ccd"), lax.axis_index("visit")
    turned[...] = jnp.zeros((32, TAIL), BF16)
    above[...] = jnp.zeros((16, PART), BF16)
    below[...] = jnp.zeros((16, PART), BF16)

    barrier = pltpu.get_barrier_semaphore()

    def greet(k, carry):
        pl.semaphore_signal(barrier, inc=1, device_id=partner(k), device_id_type=MESH)
        return carry

    bounds = [0] + [CHUNK * n + 16 for n in range(1, ROWS // CHUNK)] + [ROWS]
    image_copies = [
        pltpu.make_async_copy(
            image.at[pl.ds(a, b - a)], img.at[pl.ds(16 + a, b - a)], local_sems.at[n]
        )
        for n, (a, b) in enumerate(zip(bounds[:-1], bounds[1:]))
    ]
    wr_copies = [
        pltpu.make_async_copy(
            warp_rows.at[pl.ds(1024 * n, 1024)], wr.at[pl.ds(1024 * n, 1024)], local_sems.at[4 + n]
        )
        for n in range(2)
    ]
    wc_copy = pltpu.make_async_copy(warp_cols, wc, local_sems.at[6])
    for c in image_copies + [wr_copies[0], wc_copy, wr_copies[1]]:
        c.start()
    lax.fori_loop(1, DEVICES, greet, 0)
    img[0:16, :] = jnp.zeros((16, COLS), BF16)
    img[ROWS + 16 : ROWS + 32, :] = jnp.zeros((16, COLS), BF16)
    rp[:, :, 0:128] = jnp.zeros((NBASIS, CHUNK, 128), BF16)
    rp[:, :, COLS + 128 : COLS + 256] = jnp.zeros((NBASIS, CHUNK, 128), BF16)
    d_row = lax.broadcasted_iota(jnp.int32, (128, 160), 1) - 16 - lax.broadcasted_iota(jnp.int32, (128, 160), 0)
    d_col = lax.broadcasted_iota(jnp.int32, (512, 256), 0) - 128 - lax.broadcasted_iota(jnp.int32, (512, 256), 1)
    for b in range(NBASIS):
        sigma = widths[b]
        two_var = 2.0 * sigma * sigma
        norm = gauss_norm(two_var)
        rb[b * 128 : (b + 1) * 128, :] = gauss_at(d_row, two_var, norm).astype(BF16)
        cb[b] = gauss_at(d_col, two_var, norm).astype(BF16)

    for n in range(ROWS // CHUNK):
        image_copies[n].wait()

        def row_block(i, carry, n=n):
            y = pl.multiple_of(i * 128, 128)
            res = dot(rb[...], img[pl.ds(pl.multiple_of(n * CHUNK + y, 128), 160), :]).astype(BF16)
            for b in range(NBASIS):
                rp[b, pl.ds(y, 128), 128 : COLS + 128] = res[b * 128 : (b + 1) * 128]
            return carry

        lax.fori_loop(0, CHUNK // 128, row_block, 0)
        for q in range(VISITS):
            mixed = coefs[0] * dot(rp[0, :, q * 256 : q * 256 + 512], cb[0])
            for b in range(1, NBASIS):
                mixed = mixed + coefs[b] * dot(rp[b, :, q * 256 : q * 256 + 512], cb[b])
            matched[n * CHUNK : (n + 1) * CHUNK, q * 256 : (q + 1) * 256] = mixed.astype(BF16)

    pl.semaphore_wait(barrier, DEVICES - 1)

    def send_tags(k, carry):
        pltpu.make_async_remote_copy(
            src_ref=tags, dst_ref=tags_in.at[k], send_sem=tag_send, recv_sem=tag_recv,
            device_id=partner(k), device_id_type=MESH,
        ).start()
        return carry

    lax.fori_loop(1, DEVICES, send_tags, 0)
    tags_in[0] = tags[...]

    wc_copy.wait()
    for g in range(GROUPS):
        wr_copies[g].wait()

        def warp_block(n, carry, g=g):
            halfway = dot(wr[pl.ds(pl.multiple_of(g * 1024 + n * 256, 256), 256), :], matched[...]).astype(BF16)
            warped = dot(halfway, wc[...])
            for l in range(COLS // 128):
                for q in range(4):
                    wf[l, pl.ds((g * GROUP + n * 4 + q) * STRIDE, PIECE), :] = warped[
                        q * PIECE : (q + 1) * PIECE, l * 128 : (l + 1) * 128
                    ]
            return carry

        lax.fori_loop(0, 4, warp_block, 0)

        def pack(box, k, row, column, g=g):
            for i in range(2):
                for h in range(2):
                    rows = wf[column * 2 + h, pl.ds(g * GROUP * STRIDE + row + 32 * i, GROUP, stride=STRIDE), :]
                    box[g, pl.ds(pl.multiple_of(k * GROUP, GROUP), GROUP), (2 * i + h) * 128 : (2 * i + h + 1) * 128] = (
                        rows.astype(BF16)
                    )

        pack(inbox, 0, ccd, visit)

        def send_group(k, carry, g=g):
            to = partner(k)
            pack(outbox, k, to[0], to[1])
            rows = pl.ds(pl.multiple_of(k * GROUP, GROUP), GROUP)
            pltpu.make_async_remote_copy(
                src_ref=outbox.at[g, rows], dst_ref=inbox.at[g, rows], send_sem=out_send.at[g],
                recv_sem=out_recv.at[g, k // 16], device_id=to, device_id_type=MESH,
            ).start()
            return carry

        lax.fori_loop(1, DEVICES, send_group, 0)

    some = pl.ds(1, DEVICES - 1)
    tags_wait = pltpu.make_async_remote_copy(
        src_ref=tags_in.at[some], dst_ref=tags_in.at[some], send_sem=tag_send, recv_sem=tag_recv,
        device_id=partner(1), device_id_type=MESH,
    )
    tags_wait.wait_send()
    tags_wait.wait_recv()
    acc[...] = jnp.zeros((CELLS, WIDE), F32)
    cover[...] = jnp.zeros((40, PART), F32)
    lane = lax.broadcasted_iota(jnp.int32, (1, 128), 1) // GROUP
    cell_ids = lax.broadcasted_iota(jnp.int32, (CELLS, 256), 0)
    near_ids = lax.broadcasted_iota(jnp.int32, (40, 256), 0) + (ccd * BLOCKS - 1)
    for g in range(GROUPS):
        def sum_chunk(kb, carry, g=g):
            halves = []
            for h in range(2):
                row = jnp.zeros((1, 128), jnp.int32)
                for i in range(8):
                    row = jnp.where(lane == i, tags_in[kb * 16 + h * 8 + i, g : g + 1, :], row)
                halves.append(row)
            tag = jnp.concatenate(halves, axis=1)
            cell, weight = tag >> 3, (tag & 7).astype(F32)
            placing = jnp.where(cell_ids == cell, weight, 0.0).astype(BF16)
            cover[...] += jnp.where(near_ids == cell, weight, 0.0)
            rows = pl.ds(pl.multiple_of(kb * 256, 256), 256)
            acc[...] += dot(placing, inbox[g, rows, :])
            return carry

        for kb in range(8):
            first, last = max(1, kb * 16), (kb + 1) * 16
            rows = pl.ds(first * GROUP, (last - first) * GROUP)
            pltpu.make_async_remote_copy(
                src_ref=inbox.at[g, rows], dst_ref=inbox.at[g, rows], send_sem=out_send.at[g],
                recv_sem=out_recv.at[g, kb], device_id=partner(1), device_id_type=MESH,
            ).wait_recv()
            sum_chunk(kb, 0)
    sumbox[...] = acc[...].astype(BF16)
    cover[...] = jnp.broadcast_to(jnp.sum(cover[...], axis=1, keepdims=True), (40, PART))

    def send_sum(k, carry):
        to = patch_partner(k)
        pltpu.make_async_remote_copy(
            src_ref=sumbox.at[pl.ds(pl.multiple_of(to[0] * BLOCKS, BLOCKS), BLOCKS)], dst_ref=rows_in.at[k],
            send_sem=sum_send, recv_sem=sum_recv, device_id=to, device_id_type=MESH,
        ).start()
        return carry

    lax.fori_loop(1, CCDS, send_sum, 0)
    rows_in[0] = sumbox[pl.ds(pl.multiple_of(ccd * BLOCKS, BLOCKS), BLOCKS)]
    some = pl.ds(1, CCDS - 1)
    sums_wait = pltpu.make_async_remote_copy(
        src_ref=rows_in.at[some], dst_ref=rows_in.at[some], send_sem=sum_send, recv_sem=sum_recv,
        device_id=partner(1), device_id_type=MESH,
    )
    sums_wait.wait_recv()

    for k in range(CCDS):
        m = (k * 11) % CCDS
        z = lax.rem(ccd // 8 + (4 - m // 8), 4)
        x = lax.rem(lax.rem(ccd // 2, 4) + (4 - m // 2 % 4), 4)
        core = lax.rem(lax.rem(ccd, 2) + m % 2, 2)
        row = z * 8 + x * 2 + core
        for h in range(WIDE // 128):
            ordered[h, pl.ds(row * (BLOCKS + 1), BLOCKS), :] = rows_in[k, :, h * 128 : (h + 1) * 128].astype(F32)
    for s in range(BLOCKS):
        for h in range(WIDE // 128):
            i, l = divmod(h, 2)
            rows = ordered[h, pl.ds(s, CCDS, stride=BLOCKS + 1), :]
            y = 16 + s * PIECE + i * 32
            ext[y : y + 32, l * 128 : (l + 1) * 128] = rows.astype(BF16)

    e = lax.broadcasted_iota(jnp.int32, (32, PART), 0)
    c = lax.broadcasted_iota(jnp.int32, (32, PART), 1)
    pick = (c == jnp.where(e < 16, e + PART - 16, e - 16)).astype(F32).astype(BF16)
    edges[...] = lax.dot_general(
        pick, ext[16 : ROWS + 16, 0:PART], (((1,), (1,)), ((), ())), preferred_element_type=F32
    ).astype(BF16)
    first, last = ext.at[pl.ds(16, 16), pl.ds(0, PART)], ext.at[pl.ds(ROWS, 16), pl.ds(0, PART)]
    whole = pl.ds(128, ROWS)
    ways = [
        (1, 0, last, above),
        (-1, 0, first, below),
        (0, 1, edges.at[pl.ds(0, 16)], turned.at[pl.ds(0, 16), whole]),
        (0, -1, edges.at[pl.ds(16, 16)], turned.at[pl.ds(16, 16), whole]),
        (1, 1, edges.at[pl.ds(0, 16), pl.ds(ROWS - 128, 128)], turned.at[pl.ds(0, 16), pl.ds(0, 128)]),
        (1, -1, edges.at[pl.ds(16, 16), pl.ds(ROWS - 128, 128)], turned.at[pl.ds(16, 16), pl.ds(0, 128)]),
        (-1, 1, edges.at[pl.ds(0, 16), pl.ds(0, 128)], turned.at[pl.ds(0, 16), pl.ds(ROWS + 128, 128)]),
        (-1, -1, edges.at[pl.ds(16, 16), pl.ds(0, 128)], turned.at[pl.ds(16, 16), pl.ds(ROWS + 128, 128)]),
    ]

    def inside(c, v):
        return (c >= 0) & (c < CCDS) & (v >= 0) & (v < VISITS)

    copies = []
    for n, (dc, dv, src, dst) in enumerate(ways):
        to = (lax.rem(ccd + dc + CCDS, CCDS), lax.rem(visit + dv + VISITS, VISITS))
        copies.append(
            pltpu.make_async_remote_copy(
                src_ref=src, dst_ref=dst, send_sem=halo_send.at[n], recv_sem=halo_recv.at[n],
                device_id=to, device_id_type=MESH,
            )
        )
        pl.when(inside(ccd + dc, visit + dv))(copies[n].start)
    for n, (dc, dv, src, dst) in enumerate(ways):
        pl.when(inside(ccd - dc, visit - dv))(copies[n].wait_recv)
    ext[0:16, 0:PART] = above[...]
    ext[ROWS + 16 : ROWS + 32, 0:PART] = below[...]
    e = lax.broadcasted_iota(jnp.int32, (32, 128), 0)
    c = lax.broadcasted_iota(jnp.int32, (32, 128), 1)
    pick = (e == c).astype(F32).astype(BF16)
    ext[:, PART : PART + 128] = lax.dot_general(
        turned[...], pick, (((0,), (0,)), ((), ())), preferred_element_type=F32
    )[112 : ROWS + 144].astype(BF16)

    for n, (dc, dv, src, dst) in enumerate(ways):
        pl.when(inside(ccd + dc, visit + dv))(copies[n].wait_send)
    sums_wait.wait_send()
    for g in range(GROUPS):
        rows = pl.ds(GROUP, (DEVICES - 1) * GROUP)
        pltpu.make_async_remote_copy(
            src_ref=outbox.at[g, rows], dst_ref=outbox.at[g, rows], send_sem=out_send.at[g],
            recv_sem=out_recv.at[g, 0], device_id=partner(1), device_id_type=MESH,
        ).wait_send()


def coadd(coefs, widths, tags, image, warp_rows, warp_cols):
    smem = pl.BlockSpec(memory_space=pltpu.SMEM)
    vmem = pl.BlockSpec(memory_space=pltpu.VMEM)
    hbm = pl.BlockSpec(memory_space=pl.ANY)
    dma = pltpu.SemaphoreType.DMA
    return pl.pallas_call(
        coadd_kernel,
        out_shape=(
            jax.ShapeDtypeStruct((ROWS + 32, PART + 128), BF16),
            jax.ShapeDtypeStruct((40, PART), F32),
        ),
        in_specs=[smem, smem, vmem, hbm, hbm, hbm],
        out_specs=(vmem, vmem),
        scratch_shapes=[
            pltpu.VMEM((ROWS + 32, COLS), BF16),
            pltpu.VMEM((NBASIS, CHUNK, COLS + 256), BF16),
            pltpu.VMEM((ROWS, COLS), BF16),
            pltpu.VMEM((ROWS, ROWS), BF16),
            pltpu.VMEM((COLS, COLS), BF16),
            pltpu.VMEM((COLS // 128, BLOCKS * STRIDE, 128), F32),
            pltpu.VMEM((NBASIS * 128, 160), BF16),
            pltpu.VMEM((NBASIS, 512, 256), BF16),
            pltpu.VMEM((GROUPS, DEVICES * GROUP, WIDE), BF16),
            pltpu.VMEM((GROUPS, DEVICES * GROUP, WIDE), BF16),
            pltpu.VMEM((DEVICES, GROUPS, 128), jnp.int32),
            pltpu.VMEM((CELLS, WIDE), F32),
            pltpu.VMEM((CELLS, WIDE), BF16),
            pltpu.VMEM((CCDS, BLOCKS, WIDE), BF16),
            pltpu.VMEM((WIDE // 128, CCDS * (BLOCKS + 1), 128), F32),
            pltpu.VMEM((32, ROWS), BF16),
            pltpu.VMEM((32, TAIL), BF16),
            pltpu.VMEM((16, PART), BF16),
            pltpu.VMEM((16, PART), BF16),
            dma((7,)),
            dma,
            dma,
            dma((GROUPS,)),
            dma((GROUPS, 8)),
            dma,
            dma,
            dma((8,)),
            dma((8,)),
        ],
        compiler_params=pltpu.CompilerParams(
            vmem_limit_bytes=VMEM_LIMIT, collective_id=0, has_side_effects=True
        ),
        cost_estimate=pl.CostEstimate(flops=30_000_000_000, bytes_accessed=18 << 20, transcendentals=0),
        name="coadd",
    )(coefs, widths, tags, image, warp_rows, warp_cols)


def split_bf16(v):
    hi = v.astype(BF16)
    return hi, (v - hi.astype(F32)).astype(BF16)


def detect_kernel(place, width, cover, ext, coadd, detection):
    column0 = place[0] * PART
    sigma = width[0]
    two_var = 2.0 * sigma * sigma
    norm = gauss_norm(two_var)
    d_row = lax.broadcasted_iota(jnp.int32, (128, 160), 1) - 16 - lax.broadcasted_iota(jnp.int32, (128, 160), 0)
    row_hi, row_lo = split_bf16(gauss_at(d_row, two_var, norm))
    k = lax.broadcasted_iota(jnp.int32, (PART + 128, PART), 0)
    x = lax.broadcasted_iota(jnp.int32, (PART + 128, PART), 1)
    source = jnp.where(k < PART, k, jnp.where(k < PART + 16, k - PART - 16, jnp.where(k < PART + 32, k - 16, 4 * COLS)))
    col_hi, col_lo = split_bf16(gauss_at(source - x, two_var, norm))

    xs = lax.broadcasted_iota(jnp.int32, (1, PART), 1) + column0
    zero = jnp.zeros((1, PART), F32)
    depth_cols = zero
    r = lax.broadcasted_iota(jnp.int32, (PIECE, PART), 0)
    here = jnp.zeros((PIECE, PART), F32)
    before = jnp.zeros((PIECE, PART), F32)
    after = jnp.zeros((PIECE, PART), F32)
    for m in range(2 * HALF + 1):
        d = float(m - HALF)
        tap = jnp.exp(jnp.full((1, PART), -d * d, F32) / two_var) / norm
        sq = tap * tap
        at = xs + (m - HALF)
        depth_cols = depth_cols + jnp.where((at >= 0) & (at < COLS), sq, 0.0)
        row = r + (m - HALF)
        before = before + jnp.where(row < 0, sq, 0.0)
        after = after + jnp.where(row >= PIECE, sq, 0.0)
        here = here + jnp.where((row >= 0) & (row < PIECE), sq, 0.0)

    def block(n, carry):
        y = pl.multiple_of(n * 128, 128)
        window = ext[pl.ds(y, 160), :]
        across = dot(row_hi, window) + dot(row_lo, window)
        a_hi, a_lo = split_bf16(across)
        signal = dot(a_hi, col_hi) + (dot(a_lo, col_hi) + dot(a_hi, col_lo))
        for h in range(2):
            s = n * 2 + h
            c = cover[pl.ds(s + 1, 1), :]
            depth_rows = cover[pl.ds(s, 1), :] * before + c * here + cover[pl.ds(s + 2, 1), :] * after
            scale = lax.rsqrt(jnp.maximum(depth_rows * depth_cols, FLOOR))
            rows = pl.ds(pl.multiple_of(y + h * PIECE, PIECE), PIECE)
            detection[rows, :] = signal[h * PIECE : (h + 1) * PIECE] * scale
            own = ext[pl.ds(pl.multiple_of(y + h * PIECE + 16, 16), PIECE), 0:PART].astype(F32)
            coadd[rows, :] = own / jnp.maximum(c, 1.0)
        return carry

    lax.fori_loop(0, ROWS // 128, block, 0)


def detect(place, width, cover, ext):
    smem = pl.BlockSpec(memory_space=pltpu.SMEM)
    vmem = pl.BlockSpec(memory_space=pltpu.VMEM)
    out = jax.ShapeDtypeStruct((ROWS, PART), F32)
    return pl.pallas_call(
        detect_kernel,
        out_shape=(out, out),
        in_specs=[smem, smem, vmem, vmem],
        compiler_params=pltpu.CompilerParams(vmem_limit_bytes=VMEM_LIMIT),
        name="detect",
    )(place, width, cover, ext)


def local(image, coefs, basis_width, psf_width, warp_rows, warp_cols, visit_weight, dest_patch, dest_slot):
    cells = dest_patch.reshape(-1) * BLOCKS + dest_slot.reshape(-1)
    tags = jnp.tile((cells * 8 + visit_weight[0]).reshape(GROUPS, GROUP), (1, 128 // GROUP))
    ext, cover = coadd(coefs.reshape(-1), basis_width, tags, image[0, 0], warp_rows[0, 0], warp_cols[0, 0])
    return detect(lax.axis_index("visit")[None], psf_width, cover, ext)


def solution(mesh):
    placed = (
        P("visit", "ccd", None, None),
        P("visit", "ccd", None),
        P(),
        P(),
        P("visit", "ccd", None, None),
        P("visit", "ccd", None, None),
        P("visit"),
        P("visit", "ccd", None, None),
        P("visit", "ccd", None),
    )
    return jax.shard_map(
        local,
        mesh=mesh,
        in_specs=placed,
        out_specs=(P("ccd", "visit"), P("ccd", "visit")),
        check_vma=False,
    )
```

time: 231 us -> 124 us (0.54); the launches traced: 226 us -> 124 us
  blocking collectives: 103 us -> 0 us
  Pallas kernels: 67 us -> 118 us
  starting transfers between devices: 27 us -> 0 us
  waiting for transfers between devices: 20.2 us -> 0 us
  local copies, waits for them, and re-layouts: 4.39 us -> 1.33 us
    unnamed x1 -> x0, blocking collectives: 103 us -> none
    pallas_call x3 -> x1, Pallas kernels: 54.8 us -> 106 us  [coadd(): pl.pallas_call(coadd_kernel, out_shape=(jax.ShapeDtypeStruct((ROWS + 32,...]
    all_to_all x2 -> x0, starting transfers between devices: 17.9 us -> none  [the longest x1 12 us: local(): lax.all_to_all(outbox, ('ccd', 'visit'), split_axis=0, concat_axis=0, til...]
    all_to_all x2 -> x0, waiting for transfers between devices: 17.2 us -> none  [the longest x1 17.2 us: local(): lax.all_to_all(summed.reshape(CCDS, BLOCKS, WIDE), 'ccd', split_axis=0, c...]
    ppermute x4 -> x0, starting transfers between devices: 9.02 us -> none  [the longest x1 3.25 us: local(): above = lax.ppermute(total[ROWS - 16:], 'ccd', up)]
    ppermute x4 -> x0, waiting for transfers between devices: 3.06 us -> none  [the longest x1 1.77 us: local(): from_right = lax.ppermute(edges[:16], 'visit', left)]
  transfers between devices with their start and end apart: 6 -> 0, of which waited for: 3 -> 0; matrix products, arithmetic and copies ran while one was open for 1% -> 0% of each run, Pallas kernels for 0% -> 0%
where the time goes in v2:
time: 124 us
  Pallas kernels  118 us (95%)
  other arithmetic  2 us (2%)
  between operations  1.94 us (2%)
  local copies, waits for them, and re-layouts  1.33 us (1%)
    pallas_call x1, Pallas kernels, coadd(): pl.pallas_call(coadd_kernel, out_shape=(jax.ShapeDtypeStruct((ROWS + 32,...  106 us
    pallas_call x1, Pallas kernels, detect(): pl.pallas_call(detect_kernel, out_shape=(out, out), in_specs=[smem, smem,...  12.1 us

profile of v2, /device:TPU:1, one launch (start us, length us, event | category | flops | bytes accessed | tf_op | source)
XLA Modules:
  0.0 123.7 jit_solution(12707942575668665706)
XLA Ops:
  1.9 0.5 broadcast.22
  2.4 1.3 %reduce.7 = s32[32]{0:T(128)S(1)} reduce(s32[1,1,32]{2,1,0:T(1,128)} %param.17, s32[]{:T(128)} %broadcast.22), dimensions={0,1}, to_apply=%param.17.reduce_sub_computation.3 | reduce | bytes 260 | tf_op args[8]
  3.8 0.7 multiply_reduce_fusion
  4.4 0.1 mul.25
  4.5 0.1 reshape.29
  4.6 0.6 tile.9.tags
  5.3 106.3 %coadd.1 = (bf16[2080,384]{1,0:T(8,128)(2,1)}, f32[40,256]{1,0:T(8,128)}) custom-call(f32[3]{0:T(128)} %bitcast.10, f32[3]{0:T(128)} %widths.1, s32[2,128]{1,0:T(2,128)} %tile.9.tags, bf16[2048,1024]{1,0:T(8,128)(2,1)} %bitcast.8, bf16[2048,2048]{1,0:T(8,128)(2,1)} %bitcast.7, bf16[1024,1024]{1,0:T(8,128)(2,1)} %bitcast.9), custom_call_target="tpu_custom_call" | custom-call | flops 30000001024 | bytes 18874368 | tf_op jit(solution)/shard_map/coadd/pallas_call | solution.py:312
  111.6 12.1 %detect.1 = (f32[2048,256]{1,0:T(8,128)}, f32[2048,256]{1,0:T(8,128)}) custom-call(s32[1]{0:T(128)} %bitcast.place, f32[1]{0:T(128)S(6)} %copy.11.width, f32[40,256]{1,0:T(8,128)} %get-tuple-element.4.cover, bf16[2080,384]{1,0:T(8,128)(2,1)} %get-tuple-element.5.ext), custom_call_target="tpu_custom_call" | custom-call | tf_op jit(solution)/shard_map/detect/pallas_call | solution.py:417
  (2 shorter events, 0.0 us)

commit v3 on v2

--- a/solution.py
+++ b/solution.py
@@ -22,9 +22,12 @@
 WIDE = 2 * PART
 FLOOR = 0.05
 MESH = pl.DeviceIdType.MESH
-STRIDE = PIECE + 1
-GROUP = 16
-GROUPS = BLOCKS // GROUP
+STEPS = 4
+GROUP = PIECE // STEPS
+GROUP_ROWS = BLOCKS * GROUP
+STRIDE = GROUP + 1
+HALF_PART = PART // 2
+SOURCES = 16
 CHUNK = 512
 TAIL = ROWS + 256
 VMEM_LIMIT = 60 * 1024 * 1024
@@ -48,27 +51,39 @@
     return jnp.where(jnp.abs(d) <= HALF, jnp.exp(-df * df / two_var) / norm, 0.0)
 
 
-def shifted(steps):
-    ccd, y = lax.axis_index("ccd"), lax.axis_index("visit")
-    z, x, core = ccd // 8, lax.rem(ccd // 2, 4), lax.rem(ccd, 2)
-    z = lax.rem(z + steps // 32, 4)
-    x = lax.rem(x + lax.rem(steps // 8, 4), 4)
-    core = lax.rem(core + lax.rem(steps // 4, 2), 2)
-    y = lax.rem(y + lax.rem(steps, 4), 4)
+def place():
+    ccd = lax.axis_index("ccd")
+    return ccd // 8, lax.rem(ccd // 2, 4), lax.rem(ccd, 2), lax.axis_index("visit")
+
+
+def beyond(dz, dx, dcore, dy):
+    z, x, core, y = place()
+    return lax.rem(z + dz, 4), lax.rem(x + dx, 4), lax.rem(core + dcore, 2), lax.rem(y + dy, 4)
+
+
+def name_of(z, x, core, y):
     return z * 8 + x * 2 + core, y
 
 
-def partner(k):
-    return shifted(lax.rem(k * 59, DEVICES))
+def partner(step, n):
+    m = lax.rem(n * 11, 32)
+    dz = m // 8
+    return beyond(dz, lax.rem(step + 4 - dz, 4), lax.rem(m // 4, 2), lax.rem(m, 4))
 
 
 def patch_partner(k):
-    return shifted(4 * lax.rem(k * 11, CCDS))
+    m = lax.rem(k * 11, CCDS)
+    return beyond(m // 8, lax.rem(m // 2, 4), lax.rem(m, 2), 0)
+
+
+def first_row(z, x, core):
+    return GROUP * lax.rem(z + x, 4) + 2 * z + core
 
 
 def coadd_kernel(
-    coefs, widths, tags, image, warp_rows, warp_cols, ext, cover,
-    img, rp, matched, wr, wc, wf, rb, cb, outbox, inbox, tags_in, acc, sumbox, rows_in, ordered, edges, turned, above, below,
+    coefs, widths, weight, patches, slots, image, warp_rows, warp_cols, ext, cover,
+    img, rp, matched, wr, wc, halfway, wf, rb, cb, outbox, inbox, tags, tags_in, placing, acc, sumbox, rows_in, ordered,
+    edges, turned, above, below,
     local_sems, tag_send, tag_recv, out_send, out_recv, sum_send, sum_recv, halo_send, halo_recv,
 ):
     ccd, visit = lax.axis_index("ccd"), lax.axis_index("visit")
@@ -79,8 +94,11 @@
     barrier = pltpu.get_barrier_semaphore()
 
     def greet(k, carry):
-        pl.semaphore_signal(barrier, inc=1, device_id=partner(k), device_id_type=MESH)
+        to = name_of(*partner(k // 32, lax.rem(k, 32)))
+        pl.semaphore_signal(barrier, inc=1, device_id=to, device_id_type=MESH)
         return carry
+
+    z, x, core, _ = place()
 
     bounds = [0] + [CHUNK * n + 16 for n in range(1, ROWS // CHUNK)] + [ROWS]
     image_copies = [
@@ -89,14 +107,20 @@
         )
         for n, (a, b) in enumerate(zip(bounds[:-1], bounds[1:]))
     ]
-    wr_copies = [
+    wr_copies = []
+    for n in range(STEPS):
+        group = pl.ds(pl.multiple_of(GROUP * lax.rem(z + x + n, 4), GROUP), GROUP)
+        wr_copies.append(pltpu.make_async_copy(warp_rows.at[:, group, :], wr.at[n], local_sems.at[4 + n]))
+    wc_copies = [
         pltpu.make_async_copy(
-            warp_rows.at[pl.ds(1024 * n, 1024)], wr.at[pl.ds(1024 * n, 1024)], local_sems.at[4 + n]
+            warp_cols.at[:, pl.ds(q * PART + h * HALF_PART, HALF_PART)],
+            wc.at[h, :, pl.ds(q * HALF_PART, HALF_PART)],
+            local_sems.at[8 + h * VISITS + q],
         )
-        for n in range(2)
+        for h in range(2)
+        for q in range(VISITS)
     ]
-    wc_copy = pltpu.make_async_copy(warp_cols, wc, local_sems.at[6])
-    for c in image_copies + [wr_copies[0], wc_copy, wr_copies[1]]:
+    for c in image_copies + wr_copies[:1] + wc_copies[:4] + wr_copies[1:] + wc_copies[4:]:
         c.start()
     lax.fori_loop(1, DEVICES, greet, 0)
     img[0:16, :] = jnp.zeros((16, COLS), BF16)
@@ -129,126 +153,135 @@
                 mixed = mixed + coefs[b] * dot(rp[b, :, q * 256 : q * 256 + 512], cb[b])
             matched[n * CHUNK : (n + 1) * CHUNK, q * 256 : (q + 1) * 256] = mixed.astype(BF16)
 
+    cells = (patches[...] * BLOCKS + slots[...]) * 8 + weight[0]
+    tags[...] = jnp.concatenate([cells] * (128 // BLOCKS), axis=1)
     pl.semaphore_wait(barrier, DEVICES - 1)
 
     def send_tags(k, carry):
+        to = name_of(*partner(k // 32, lax.rem(k, 32)))
         pltpu.make_async_remote_copy(
             src_ref=tags, dst_ref=tags_in.at[k], send_sem=tag_send, recv_sem=tag_recv,
-            device_id=partner(k), device_id_type=MESH,
+            device_id=to, device_id_type=MESH,
         ).start()
         return carry
 
     lax.fori_loop(1, DEVICES, send_tags, 0)
     tags_in[0] = tags[...]
 
-    wc_copy.wait()
-    for g in range(GROUPS):
-        wr_copies[g].wait()
-
-        def warp_block(n, carry, g=g):
-            halfway = dot(wr[pl.ds(pl.multiple_of(g * 1024 + n * 256, 256), 256), :], matched[...]).astype(BF16)
-            warped = dot(halfway, wc[...])
-            for l in range(COLS // 128):
-                for q in range(4):
-                    wf[l, pl.ds((g * GROUP + n * 4 + q) * STRIDE, PIECE), :] = warped[
-                        q * PIECE : (q + 1) * PIECE, l * 128 : (l + 1) * 128
-                    ]
+    def pack(box, h, k, to):
+        row = 2 * to[0] + to[2]
+        for i in range(2):
+            rows = wf[to[3], pl.ds(row + 8 * i, BLOCKS, stride=STRIDE), :]
+            box[h, pl.ds(pl.multiple_of(k * BLOCKS, BLOCKS), BLOCKS), i * 128 : (i + 1) * 128] = rows.astype(BF16)
+
+    for h in range(2):
+        for c in wc_copies[h * VISITS : (h + 1) * VISITS]:
+            c.wait()
+
+        def warp_step(n, carry, h=h):
+            if h == 0:
+                half = dot(wr[n].reshape(GROUP_ROWS, ROWS), matched[...]).astype(BF16)
+                halfway[n] = half
+            else:
+                half = halfway[n]
+            warped = dot(half, wc[h])
+            for q in range(VISITS):
+                for p in range(BLOCKS):
+                    wf[q, pl.ds(p * STRIDE, GROUP), :] = warped[p * GROUP : (p + 1) * GROUP, q * 128 : (q + 1) * 128]
+
+            def send(t, carry):
+                k = n * 32 + t
+                to = partner(n, t)
+                pack(outbox, h, k, to)
+                rows = pl.ds(pl.multiple_of(k * BLOCKS, BLOCKS), BLOCKS)
+                pltpu.make_async_remote_copy(
+                    src_ref=outbox.at[h, rows], dst_ref=inbox.at[h, rows], send_sem=out_send.at[h],
+                    recv_sem=out_recv.at[h, k // SOURCES], device_id=name_of(*to), device_id_type=MESH,
+                ).start()
+                return carry
+
+            lax.fori_loop(jnp.where(n == 0, 1, 0), 32, send, 0)
             return carry
 
-        lax.fori_loop(0, 4, warp_block, 0)
-
-        def pack(box, k, row, column, g=g):
-            for i in range(2):
-                for h in range(2):
-                    rows = wf[column * 2 + h, pl.ds(g * GROUP * STRIDE + row + 32 * i, GROUP, stride=STRIDE), :]
-                    box[g, pl.ds(pl.multiple_of(k * GROUP, GROUP), GROUP), (2 * i + h) * 128 : (2 * i + h + 1) * 128] = (
-                        rows.astype(BF16)
-                    )
-
-        pack(inbox, 0, ccd, visit)
-
-        def send_group(k, carry, g=g):
-            to = partner(k)
-            pack(outbox, k, to[0], to[1])
-            rows = pl.ds(pl.multiple_of(k * GROUP, GROUP), GROUP)
-            pltpu.make_async_remote_copy(
-                src_ref=outbox.at[g, rows], dst_ref=inbox.at[g, rows], send_sem=out_send.at[g],
-                recv_sem=out_recv.at[g, k // 16], device_id=to, device_id_type=MESH,
-            ).start()
-            return carry
-
-        lax.fori_loop(1, DEVICES, send_group, 0)
+        for n in range(STEPS):
+            if h == 0:
+                wr_copies[n].wait()
+            if n == 0:
+                warp_step(0, 0)
+                pack(inbox, h, 0, place())
+            else:
+                warp_step(n, 0)
 
     some = pl.ds(1, DEVICES - 1)
     tags_wait = pltpu.make_async_remote_copy(
         src_ref=tags_in.at[some], dst_ref=tags_in.at[some], send_sem=tag_send, recv_sem=tag_recv,
-        device_id=partner(1), device_id_type=MESH,
+        device_id=name_of(*partner(0, 1)), device_id_type=MESH,
     )
     tags_wait.wait_send()
     tags_wait.wait_recv()
-    acc[...] = jnp.zeros((CELLS, WIDE), F32)
-    cover[...] = jnp.zeros((40, PART), F32)
-    lane = lax.broadcasted_iota(jnp.int32, (1, 128), 1) // GROUP
-    cell_ids = lax.broadcasted_iota(jnp.int32, (CELLS, 256), 0)
-    near_ids = lax.broadcasted_iota(jnp.int32, (40, 256), 0) + (ccd * BLOCKS - 1)
-    for g in range(GROUPS):
-        def sum_chunk(kb, carry, g=g):
-            halves = []
-            for h in range(2):
-                row = jnp.zeros((1, 128), jnp.int32)
-                for i in range(8):
-                    row = jnp.where(lane == i, tags_in[kb * 16 + h * 8 + i, g : g + 1, :], row)
-                halves.append(row)
-            tag = jnp.concatenate(halves, axis=1)
-            cell, weight = tag >> 3, (tag & 7).astype(F32)
-            placing = jnp.where(cell_ids == cell, weight, 0.0).astype(BF16)
-            cover[...] += jnp.where(near_ids == cell, weight, 0.0)
-            rows = pl.ds(pl.multiple_of(kb * 256, 256), 256)
-            acc[...] += dot(placing, inbox[g, rows, :])
+    lane = lax.broadcasted_iota(jnp.int32, (1, 128), 1) // BLOCKS
+    cell_ids = lax.broadcasted_iota(jnp.int32, (CELLS, 128), 0)
+    near_ids = lax.broadcasted_iota(jnp.int32, (40, 128), 0) + (ccd * BLOCKS - 1)
+
+    def place_some(n, covered):
+        tag = tags_in[n * 4]
+        for i in range(1, 4):
+            tag = jnp.where(lane == i, tags_in[n * 4 + i], tag)
+        cell, heavy = tag >> 3, (tag & 7).astype(F32)
+        placing[n // 4, :, pl.ds(pl.multiple_of(lax.rem(n, 4) * 128, 128), 128)] = jnp.where(cell_ids == cell, heavy, 0.0).astype(BF16)
+        return covered + jnp.where(near_ids == cell, heavy, 0.0)
+
+    covered = lax.fori_loop(0, DEVICES // 4, place_some, jnp.zeros((40, 128), F32))
+    cover[...] = jnp.broadcast_to(jnp.sum(covered, axis=1, keepdims=True), (40, PART))
+
+    for h in range(2):
+        for b in range(DEVICES // SOURCES):
+            first, last = max(1, b * SOURCES), (b + 1) * SOURCES
+            rows = pl.ds(first * BLOCKS, (last - first) * BLOCKS)
+            pltpu.make_async_remote_copy(
+                src_ref=inbox.at[h, rows], dst_ref=inbox.at[h, rows], send_sem=out_send.at[h],
+                recv_sem=out_recv.at[h, b], device_id=name_of(*partner(0, 1)), device_id_type=MESH,
+            ).wait_recv()
+            part = dot(placing[b], inbox[h, b * SOURCES * BLOCKS : last * BLOCKS, :])
+            if b == 0:
+                acc[...] = part
+            elif b < DEVICES // SOURCES - 1:
+                acc[...] += part
+            else:
+                sumbox[h] = (acc[...] + part).astype(BF16)
+
+        def send_sum(k, carry, h=h):
+            to = name_of(*patch_partner(k))
+            pltpu.make_async_remote_copy(
+                src_ref=sumbox.at[h, pl.ds(pl.multiple_of(to[0] * BLOCKS, BLOCKS), BLOCKS)], dst_ref=rows_in.at[h, k],
+                send_sem=sum_send.at[h], recv_sem=sum_recv.at[h], device_id=to, device_id_type=MESH,
+            ).start()
             return carry
 
-        for kb in range(8):
-            first, last = max(1, kb * 16), (kb + 1) * 16
-            rows = pl.ds(first * GROUP, (last - first) * GROUP)
+        lax.fori_loop(1, CCDS, send_sum, 0)
+        rows_in[h, 0] = sumbox[h, pl.ds(pl.multiple_of(ccd * BLOCKS, BLOCKS), BLOCKS)]
+
+    some = pl.ds(1, CCDS - 1)
+    sums_waits = []
+    for h in range(2):
+        sums_waits.append(
             pltpu.make_async_remote_copy(
-                src_ref=inbox.at[g, rows], dst_ref=inbox.at[g, rows], send_sem=out_send.at[g],
-                recv_sem=out_recv.at[g, kb], device_id=partner(1), device_id_type=MESH,
-            ).wait_recv()
-            sum_chunk(kb, 0)
-    sumbox[...] = acc[...].astype(BF16)
-    cover[...] = jnp.broadcast_to(jnp.sum(cover[...], axis=1, keepdims=True), (40, PART))
-
-    def send_sum(k, carry):
-        to = patch_partner(k)
-        pltpu.make_async_remote_copy(
-            src_ref=sumbox.at[pl.ds(pl.multiple_of(to[0] * BLOCKS, BLOCKS), BLOCKS)], dst_ref=rows_in.at[k],
-            send_sem=sum_send, recv_sem=sum_recv, device_id=to, device_id_type=MESH,
-        ).start()
-        return carry
-
-    lax.fori_loop(1, CCDS, send_sum, 0)
-    rows_in[0] = sumbox[pl.ds(pl.multiple_of(ccd * BLOCKS, BLOCKS), BLOCKS)]
-    some = pl.ds(1, CCDS - 1)
-    sums_wait = pltpu.make_async_remote_copy(
-        src_ref=rows_in.at[some], dst_ref=rows_in.at[some], send_sem=sum_send, recv_sem=sum_recv,
-        device_id=partner(1), device_id_type=MESH,
-    )
-    sums_wait.wait_recv()
-
-    for k in range(CCDS):
-        m = (k * 11) % CCDS
-        z = lax.rem(ccd // 8 + (4 - m // 8), 4)
-        x = lax.rem(lax.rem(ccd // 2, 4) + (4 - m // 2 % 4), 4)
-        core = lax.rem(lax.rem(ccd, 2) + m % 2, 2)
-        row = z * 8 + x * 2 + core
-        for h in range(WIDE // 128):
-            ordered[h, pl.ds(row * (BLOCKS + 1), BLOCKS), :] = rows_in[k, :, h * 128 : (h + 1) * 128].astype(F32)
-    for s in range(BLOCKS):
-        for h in range(WIDE // 128):
-            i, l = divmod(h, 2)
-            rows = ordered[h, pl.ds(s, CCDS, stride=BLOCKS + 1), :]
-            y = 16 + s * PIECE + i * 32
-            ext[y : y + 32, l * 128 : (l + 1) * 128] = rows.astype(BF16)
+                src_ref=rows_in.at[h, some], dst_ref=rows_in.at[h, some], send_sem=sum_send.at[h],
+                recv_sem=sum_recv.at[h], device_id=name_of(*partner(0, 1)), device_id_type=MESH,
+            )
+        )
+        sums_waits[h].wait_recv()
+        for k in range(CCDS):
+            m = (k * 11) % CCDS
+            sz, sx, score, _ = beyond((4 - m // 8) % 4, (4 - m // 2 % 4) % 4, m % 2, 0)
+            row = first_row(sz, sx, score)
+            for i in range(2):
+                ordered[h, pl.ds((row + 8 * i) * (BLOCKS + 1), BLOCKS), :] = rows_in[
+                    h, k, :, i * 128 : (i + 1) * 128
+                ].astype(F32)
+        for p in range(BLOCKS):
+            rows = ordered[h, pl.ds(p, PIECE, stride=BLOCKS + 1), :]
+            ext[16 + p * PIECE : 16 + (p + 1) * PIECE, h * 128 : (h + 1) * 128] = rows.astype(BF16)
 
     e = lax.broadcasted_iota(jnp.int32, (32, PART), 0)
     c = lax.broadcasted_iota(jnp.int32, (32, PART), 1)
@@ -295,16 +328,16 @@
 
     for n, (dc, dv, src, dst) in enumerate(ways):
         pl.when(inside(ccd + dc, visit + dv))(copies[n].wait_send)
-    sums_wait.wait_send()
-    for g in range(GROUPS):
-        rows = pl.ds(GROUP, (DEVICES - 1) * GROUP)
+    for h in range(2):
+        sums_waits[h].wait_send()
+        rows = pl.ds(BLOCKS, (DEVICES - 1) * BLOCKS)
         pltpu.make_async_remote_copy(
-            src_ref=outbox.at[g, rows], dst_ref=outbox.at[g, rows], send_sem=out_send.at[g],
-            recv_sem=out_recv.at[g, 0], device_id=partner(1), device_id_type=MESH,
+            src_ref=outbox.at[h, rows], dst_ref=outbox.at[h, rows], send_sem=out_send.at[h],
+            recv_sem=out_recv.at[h, 0], device_id=name_of(*partner(0, 1)), device_id_type=MESH,
         ).wait_send()
 
 
-def coadd(coefs, widths, tags, image, warp_rows, warp_cols):
+def coadd(coefs, widths, weight, patches, slots, image, warp_rows, warp_cols):
     smem = pl.BlockSpec(memory_space=pltpu.SMEM)
     vmem = pl.BlockSpec(memory_space=pltpu.VMEM)
     hbm = pl.BlockSpec(memory_space=pl.ANY)
@@ -315,35 +348,38 @@
             jax.ShapeDtypeStruct((ROWS + 32, PART + 128), BF16),
             jax.ShapeDtypeStruct((40, PART), F32),
         ),
-        in_specs=[smem, smem, vmem, hbm, hbm, hbm],
+        in_specs=[smem, smem, smem, vmem, vmem, hbm, hbm, hbm],
         out_specs=(vmem, vmem),
         scratch_shapes=[
             pltpu.VMEM((ROWS + 32, COLS), BF16),
             pltpu.VMEM((NBASIS, CHUNK, COLS + 256), BF16),
             pltpu.VMEM((ROWS, COLS), BF16),
-            pltpu.VMEM((ROWS, ROWS), BF16),
-            pltpu.VMEM((COLS, COLS), BF16),
-            pltpu.VMEM((COLS // 128, BLOCKS * STRIDE, 128), F32),
+            pltpu.VMEM((STEPS, BLOCKS, GROUP, ROWS), BF16),
+            pltpu.VMEM((2, COLS, COLS // 2), BF16),
+            pltpu.VMEM((STEPS, GROUP_ROWS, COLS), BF16),
+            pltpu.VMEM((VISITS, BLOCKS * STRIDE, 128), F32),
             pltpu.VMEM((NBASIS * 128, 160), BF16),
             pltpu.VMEM((NBASIS, 512, 256), BF16),
-            pltpu.VMEM((GROUPS, DEVICES * GROUP, WIDE), BF16),
-            pltpu.VMEM((GROUPS, DEVICES * GROUP, WIDE), BF16),
-            pltpu.VMEM((DEVICES, GROUPS, 128), jnp.int32),
-            pltpu.VMEM((CELLS, WIDE), F32),
-            pltpu.VMEM((CELLS, WIDE), BF16),
-            pltpu.VMEM((CCDS, BLOCKS, WIDE), BF16),
-            pltpu.VMEM((WIDE // 128, CCDS * (BLOCKS + 1), 128), F32),
+            pltpu.VMEM((2, PIECES, PART), BF16),
+            pltpu.VMEM((2, PIECES, PART), BF16),
+            pltpu.VMEM((1, 128), jnp.int32),
+            pltpu.VMEM((DEVICES, 1, 128), jnp.int32),
+            pltpu.VMEM((DEVICES // SOURCES, CELLS, SOURCES * BLOCKS), BF16),
+            pltpu.VMEM((CELLS, PART), F32),
+            pltpu.VMEM((2, CELLS, PART), BF16),
+            pltpu.VMEM((2, CCDS, BLOCKS, PART), BF16),
+            pltpu.VMEM((2, PIECE * (BLOCKS + 1), 128), F32),
             pltpu.VMEM((32, ROWS), BF16),
             pltpu.VMEM((32, TAIL), BF16),
             pltpu.VMEM((16, PART), BF16),
             pltpu.VMEM((16, PART), BF16),
-            dma((7,)),
+            dma((16,)),
             dma,
             dma,
-            dma((GROUPS,)),
-            dma((GROUPS, 8)),
-            dma,
-            dma,
+            dma((2,)),
+            dma((2, DEVICES // SOURCES)),
+            dma((2,)),
+            dma((2,)),
             dma((8,)),
             dma((8,)),
         ],
@@ -352,7 +388,7 @@
         ),
         cost_estimate=pl.CostEstimate(flops=30_000_000_000, bytes_accessed=18 << 20, transcendentals=0),
         name="coadd",
-    )(coefs, widths, tags, image, warp_rows, warp_cols)
+    )(coefs, widths, weight, patches, slots, image, warp_rows, warp_cols)
 
 
 def split_bf16(v):
@@ -424,9 +460,10 @@
 
 
 def local(image, coefs, basis_width, psf_width, warp_rows, warp_cols, visit_weight, dest_patch, dest_slot):
-    cells = dest_patch.reshape(-1) * BLOCKS + dest_slot.reshape(-1)
-    tags = jnp.tile((cells * 8 + visit_weight[0]).reshape(GROUPS, GROUP), (1, 128 // GROUP))
-    ext, cover = coadd(coefs.reshape(-1), basis_width, tags, image[0, 0], warp_rows[0, 0], warp_cols[0, 0])
+    ext, cover = coadd(
+        coefs.reshape(-1), basis_width, visit_weight, dest_patch.reshape(1, BLOCKS), dest_slot.reshape(1, BLOCKS),
+        image[0, 0], warp_rows.reshape(BLOCKS, PIECE, ROWS), warp_cols[0, 0],
+    )
     return detect(lax.axis_index("visit")[None], psf_width, cover, ext)
 
 

time: 124 us -> 116 us (0.935)
  Pallas kernels: 118 us -> 114 us
  other arithmetic: 2 us -> 0 us
  local copies, waits for them, and re-layouts: 1.33 us -> 0 us
    pallas_call x1, Pallas kernels: 106 us -> 102 us  [coadd(): pl.pallas_call(coadd_kernel, out_shape=(jax.ShapeDtypeStruct((ROWS + 32,...]
    unnamed x1 -> x0, other arithmetic: 1.32 us -> none
where the time goes in v3:
time: 116 us
  Pallas kernels  114 us (98%)
  between operations  1.94 us (2%)
    pallas_call x1, Pallas kernels, coadd(): pl.pallas_call(coadd_kernel, out_shape=(jax.ShapeDtypeStruct((ROWS + 32,...  102 us
    pallas_call x1, Pallas kernels, detect(): pl.pallas_call(detect_kernel, out_shape=(out, out), in_specs=[smem, smem,...  12.1 us

profile of v3, /device:TPU:1, one launch (start us, length us, event | category | flops | bytes accessed | tf_op | source)
XLA Modules:
  0.0 115.6 jit_solution(14666268447952433139)
XLA Ops:
  1.9 101.6 %coadd.1 = (bf16[2080,384]{1,0:T(8,128)(2,1)}, f32[40,256]{1,0:T(8,128)}) custom-call(f32[3]{0:T(128)} %bitcast.10, f32[3]{0:T(128)} %widths.1, s32[1]{0:T(128)S(6)} %copy.12.weight, s32[1,32]{1,0:T(1,128)} %bitcast.11, s32[1,32]{1,0:T(1,128)} %bitcast.12, bf16[2048,1024]{1,0:T(8,128)(2,1)} %bitcast.8, bf16[32,64,2048]{2,1,0:T(8,128)(2,1)} %bitcast.7, ...), custom_call_target="tpu_custom_call" | custom-call | flops 30000001024 | bytes 18874368 | tf_op jit(solution)/shard_map/coadd/pallas_call | solution.py:345
  103.5 12.1 %detect.1 = (f32[2048,256]{1,0:T(8,128)}, f32[2048,256]{1,0:T(8,128)}) custom-call(s32[1]{0:T(128)} %bitcast.place, f32[1]{0:T(128)S(6)} %copy.11.width, f32[40,256]{1,0:T(8,128)} %get-tuple-element.4.cover, bf16[2080,384]{1,0:T(8,128)(2,1)} %get-tuple-element.5.ext), custom_call_target="tpu_custom_call" | custom-call | tf_op jit(solution)/shard_map/detect/pallas_call | solution.py:453

commit v4 on v3

--- a/solution.py
+++ b/solution.py
@@ -29,6 +29,7 @@
 HALF_PART = PART // 2
 SOURCES = 16
 CHUNK = 512
+DETECT_ROWS = 512
 TAIL = ROWS + 256
 VMEM_LIMIT = 60 * 1024 * 1024
 
@@ -53,11 +54,11 @@
 
 def place():
     ccd = lax.axis_index("ccd")
-    return ccd // 8, lax.rem(ccd // 2, 4), lax.rem(ccd, 2), lax.axis_index("visit")
-
-
-def beyond(dz, dx, dcore, dy):
-    z, x, core, y = place()
+    return lax.div(ccd, 8), lax.rem(lax.div(ccd, 2), 4), lax.rem(ccd, 2), lax.axis_index("visit")
+
+
+def beyond(here, dz, dx, dcore, dy):
+    z, x, core, y = here
     return lax.rem(z + dz, 4), lax.rem(x + dx, 4), lax.rem(core + dcore, 2), lax.rem(y + dy, 4)
 
 
@@ -65,15 +66,15 @@
     return z * 8 + x * 2 + core, y
 
 
-def partner(step, n):
+def partner(here, step, n):
     m = lax.rem(n * 11, 32)
-    dz = m // 8
-    return beyond(dz, lax.rem(step + 4 - dz, 4), lax.rem(m // 4, 2), lax.rem(m, 4))
-
-
-def patch_partner(k):
+    dz = lax.div(m, 8)
+    return beyond(here, dz, lax.rem(step + 4 - dz, 4), lax.rem(lax.div(m, 4), 2), lax.rem(m, 4))
+
+
+def patch_partner(here, k):
     m = lax.rem(k * 11, CCDS)
-    return beyond(m // 8, lax.rem(m // 2, 4), lax.rem(m, 2), 0)
+    return beyond(here, lax.div(m, 8), lax.rem(lax.div(m, 2), 4), lax.rem(m, 2), 0)
 
 
 def first_row(z, x, core):
@@ -94,11 +95,14 @@
     barrier = pltpu.get_barrier_semaphore()
 
     def greet(k, carry):
-        to = name_of(*partner(k // 32, lax.rem(k, 32)))
-        pl.semaphore_signal(barrier, inc=1, device_id=to, device_id_type=MESH)
+        to = lax.rem(me + k, DEVICES)
+        pl.semaphore_signal(barrier, inc=1, device_id=(lax.div(to, VISITS), lax.rem(to, VISITS)), device_id_type=MESH)
         return carry
 
-    z, x, core, _ = place()
+    here = place()
+    z, x, core, _ = here
+    me = ccd * VISITS + visit
+    other = (lax.rem(ccd + 1, CCDS), visit)
 
     bounds = [0] + [CHUNK * n + 16 for n in range(1, ROWS // CHUNK)] + [ROWS]
     image_copies = [
@@ -146,7 +150,7 @@
                 rp[b, pl.ds(y, 128), 128 : COLS + 128] = res[b * 128 : (b + 1) * 128]
             return carry
 
-        lax.fori_loop(0, CHUNK // 128, row_block, 0)
+        lax.fori_loop(0, CHUNK // 128, row_block, 0, unroll=True)
         for q in range(VISITS):
             mixed = coefs[0] * dot(rp[0, :, q * 256 : q * 256 + 512], cb[0])
             for b in range(1, NBASIS):
@@ -157,15 +161,6 @@
     tags[...] = jnp.concatenate([cells] * (128 // BLOCKS), axis=1)
     pl.semaphore_wait(barrier, DEVICES - 1)
 
-    def send_tags(k, carry):
-        to = name_of(*partner(k // 32, lax.rem(k, 32)))
-        pltpu.make_async_remote_copy(
-            src_ref=tags, dst_ref=tags_in.at[k], send_sem=tag_send, recv_sem=tag_recv,
-            device_id=to, device_id_type=MESH,
-        ).start()
-        return carry
-
-    lax.fori_loop(1, DEVICES, send_tags, 0)
     tags_in[0] = tags[...]
 
     def pack(box, h, k, to):
@@ -191,31 +186,35 @@
 
             def send(t, carry):
                 k = n * 32 + t
-                to = partner(n, t)
+                to = partner(here, n, t)
+                device = name_of(*to)
                 pack(outbox, h, k, to)
                 rows = pl.ds(pl.multiple_of(k * BLOCKS, BLOCKS), BLOCKS)
                 pltpu.make_async_remote_copy(
                     src_ref=outbox.at[h, rows], dst_ref=inbox.at[h, rows], send_sem=out_send.at[h],
-                    recv_sem=out_recv.at[h, k // SOURCES], device_id=name_of(*to), device_id_type=MESH,
+                    recv_sem=out_recv.at[h, lax.div(k, SOURCES)], device_id=device, device_id_type=MESH,
                 ).start()
+                if h == 0:
+                    pltpu.make_async_remote_copy(
+                        src_ref=tags, dst_ref=tags_in.at[k], send_sem=tag_send, recv_sem=tag_recv,
+                        device_id=device, device_id_type=MESH,
+                    ).start()
                 return carry
 
-            lax.fori_loop(jnp.where(n == 0, 1, 0), 32, send, 0)
+            lax.fori_loop(1 if n == 0 else 0, 32, send, 0)
             return carry
 
         for n in range(STEPS):
             if h == 0:
                 wr_copies[n].wait()
+            warp_step(n, 0)
             if n == 0:
-                warp_step(0, 0)
-                pack(inbox, h, 0, place())
-            else:
-                warp_step(n, 0)
+                pack(inbox, h, 0, here)
 
     some = pl.ds(1, DEVICES - 1)
     tags_wait = pltpu.make_async_remote_copy(
         src_ref=tags_in.at[some], dst_ref=tags_in.at[some], send_sem=tag_send, recv_sem=tag_recv,
-        device_id=name_of(*partner(0, 1)), device_id_type=MESH,
+        device_id=other, device_id_type=MESH,
     )
     tags_wait.wait_send()
     tags_wait.wait_recv()
@@ -240,7 +239,7 @@
             rows = pl.ds(first * BLOCKS, (last - first) * BLOCKS)
             pltpu.make_async_remote_copy(
                 src_ref=inbox.at[h, rows], dst_ref=inbox.at[h, rows], send_sem=out_send.at[h],
-                recv_sem=out_recv.at[h, b], device_id=name_of(*partner(0, 1)), device_id_type=MESH,
+                recv_sem=out_recv.at[h, b], device_id=other, device_id_type=MESH,
             ).wait_recv()
             part = dot(placing[b], inbox[h, b * SOURCES * BLOCKS : last * BLOCKS, :])
             if b == 0:
@@ -251,7 +250,7 @@
                 sumbox[h] = (acc[...] + part).astype(BF16)
 
         def send_sum(k, carry, h=h):
-            to = name_of(*patch_partner(k))
+            to = name_of(*patch_partner(here, k))
             pltpu.make_async_remote_copy(
                 src_ref=sumbox.at[h, pl.ds(pl.multiple_of(to[0] * BLOCKS, BLOCKS), BLOCKS)], dst_ref=rows_in.at[h, k],
                 send_sem=sum_send.at[h], recv_sem=sum_recv.at[h], device_id=to, device_id_type=MESH,
@@ -261,50 +260,19 @@
         lax.fori_loop(1, CCDS, send_sum, 0)
         rows_in[h, 0] = sumbox[h, pl.ds(pl.multiple_of(ccd * BLOCKS, BLOCKS), BLOCKS)]
 
-    some = pl.ds(1, CCDS - 1)
-    sums_waits = []
-    for h in range(2):
-        sums_waits.append(
-            pltpu.make_async_remote_copy(
-                src_ref=rows_in.at[h, some], dst_ref=rows_in.at[h, some], send_sem=sum_send.at[h],
-                recv_sem=sum_recv.at[h], device_id=name_of(*partner(0, 1)), device_id_type=MESH,
-            )
-        )
-        sums_waits[h].wait_recv()
-        for k in range(CCDS):
-            m = (k * 11) % CCDS
-            sz, sx, score, _ = beyond((4 - m // 8) % 4, (4 - m // 2 % 4) % 4, m % 2, 0)
-            row = first_row(sz, sx, score)
-            for i in range(2):
-                ordered[h, pl.ds((row + 8 * i) * (BLOCKS + 1), BLOCKS), :] = rows_in[
-                    h, k, :, i * 128 : (i + 1) * 128
-                ].astype(F32)
-        for p in range(BLOCKS):
-            rows = ordered[h, pl.ds(p, PIECE, stride=BLOCKS + 1), :]
-            ext[16 + p * PIECE : 16 + (p + 1) * PIECE, h * 128 : (h + 1) * 128] = rows.astype(BF16)
-
-    e = lax.broadcasted_iota(jnp.int32, (32, PART), 0)
-    c = lax.broadcasted_iota(jnp.int32, (32, PART), 1)
-    pick = (c == jnp.where(e < 16, e + PART - 16, e - 16)).astype(F32).astype(BF16)
-    edges[...] = lax.dot_general(
-        pick, ext[16 : ROWS + 16, 0:PART], (((1,), (1,)), ((), ())), preferred_element_type=F32
-    ).astype(BF16)
     first, last = ext.at[pl.ds(16, 16), pl.ds(0, PART)], ext.at[pl.ds(ROWS, 16), pl.ds(0, PART)]
-    whole = pl.ds(128, ROWS)
+    from_left, from_right = pl.ds(0, 16), pl.ds(16, 16)
+    whole, head, tail = pl.ds(128, ROWS), pl.ds(0, 128), pl.ds(ROWS + 128, 128)
     ways = [
+        (0, -1, edges.at[0], turned.at[from_right, whole]),
+        (1, -1, edges.at[0, :, pl.ds(ROWS - 128, 128)], turned.at[from_right, head]),
+        (-1, -1, edges.at[0, :, pl.ds(0, 128)], turned.at[from_right, tail]),
+        (0, 1, edges.at[1], turned.at[from_left, whole]),
+        (1, 1, edges.at[1, :, pl.ds(ROWS - 128, 128)], turned.at[from_left, head]),
+        (-1, 1, edges.at[1, :, pl.ds(0, 128)], turned.at[from_left, tail]),
         (1, 0, last, above),
         (-1, 0, first, below),
-        (0, 1, edges.at[pl.ds(0, 16)], turned.at[pl.ds(0, 16), whole]),
-        (0, -1, edges.at[pl.ds(16, 16)], turned.at[pl.ds(16, 16), whole]),
-        (1, 1, edges.at[pl.ds(0, 16), pl.ds(ROWS - 128, 128)], turned.at[pl.ds(0, 16), pl.ds(0, 128)]),
-        (1, -1, edges.at[pl.ds(16, 16), pl.ds(ROWS - 128, 128)], turned.at[pl.ds(16, 16), pl.ds(0, 128)]),
-        (-1, 1, edges.at[pl.ds(0, 16), pl.ds(0, 128)], turned.at[pl.ds(0, 16), pl.ds(ROWS + 128, 128)]),
-        (-1, -1, edges.at[pl.ds(16, 16), pl.ds(0, 128)], turned.at[pl.ds(16, 16), pl.ds(ROWS + 128, 128)]),
     ]
-
-    def inside(c, v):
-        return (c >= 0) & (c < CCDS) & (v >= 0) & (v < VISITS)
-
     copies = []
     for n, (dc, dv, src, dst) in enumerate(ways):
         to = (lax.rem(ccd + dc + CCDS, CCDS), lax.rem(visit + dv + VISITS, VISITS))
@@ -314,7 +282,40 @@
                 device_id=to, device_id_type=MESH,
             )
         )
-        pl.when(inside(ccd + dc, visit + dv))(copies[n].start)
+
+    def inside(c, v):
+        return (c >= 0) & (c < CCDS) & (v >= 0) & (v < VISITS)
+
+    some = pl.ds(1, CCDS - 1)
+    e = lax.broadcasted_iota(jnp.int32, (16, 128), 0)
+    c = lax.broadcasted_iota(jnp.int32, (16, 128), 1)
+    sums_waits = []
+    for h in range(2):
+        sums_waits.append(
+            pltpu.make_async_remote_copy(
+                src_ref=rows_in.at[h, some], dst_ref=rows_in.at[h, some], send_sem=sum_send.at[h],
+                recv_sem=sum_recv.at[h], device_id=other, device_id_type=MESH,
+            )
+        )
+        sums_waits[h].wait_recv()
+        for k in range(CCDS):
+            m = (k * 11) % CCDS
+            sz, sx, score, _ = beyond(here, (4 - m // 8) % 4, (4 - m // 2 % 4) % 4, m % 2, 0)
+            row = first_row(sz, sx, score)
+            for i in range(2):
+                ordered[h, pl.ds((row + 8 * i) * (BLOCKS + 1), BLOCKS), :] = rows_in[
+                    h, k, :, i * 128 : (i + 1) * 128
+                ].astype(F32)
+        for p in range(BLOCKS):
+            rows = ordered[h, pl.ds(p, PIECE, stride=BLOCKS + 1), :]
+            ext[16 + p * PIECE : 16 + (p + 1) * PIECE, h * 128 : (h + 1) * 128] = rows.astype(BF16)
+        pick = (c == e + 112 * h).astype(F32).astype(BF16)
+        edges[h] = lax.dot_general(
+            pick, ext[16 : ROWS + 16, h * 128 : (h + 1) * 128], (((1,), (1,)), ((), ())), preferred_element_type=F32
+        ).astype(BF16)
+        for n in (range(3) if h == 0 else range(3, 8)):
+            dc, dv = ways[n][:2]
+            pl.when(inside(ccd + dc, visit + dv))(copies[n].start)
     for n, (dc, dv, src, dst) in enumerate(ways):
         pl.when(inside(ccd - dc, visit - dv))(copies[n].wait_recv)
     ext[0:16, 0:PART] = above[...]
@@ -333,7 +334,7 @@
         rows = pl.ds(BLOCKS, (DEVICES - 1) * BLOCKS)
         pltpu.make_async_remote_copy(
             src_ref=outbox.at[h, rows], dst_ref=outbox.at[h, rows], send_sem=out_send.at[h],
-            recv_sem=out_recv.at[h, 0], device_id=name_of(*partner(0, 1)), device_id_type=MESH,
+            recv_sem=out_recv.at[h, 0], device_id=other, device_id_type=MESH,
         ).wait_send()
 
 
@@ -369,7 +370,7 @@
             pltpu.VMEM((2, CELLS, PART), BF16),
             pltpu.VMEM((2, CCDS, BLOCKS, PART), BF16),
             pltpu.VMEM((2, PIECE * (BLOCKS + 1), 128), F32),
-            pltpu.VMEM((32, ROWS), BF16),
+            pltpu.VMEM((2, 16, ROWS), BF16),
             pltpu.VMEM((32, TAIL), BF16),
             pltpu.VMEM((16, PART), BF16),
             pltpu.VMEM((16, PART), BF16),
@@ -396,64 +397,89 @@
     return hi, (v - hi.astype(F32)).astype(BF16)
 
 
-def detect_kernel(place, width, cover, ext, coadd, detection):
-    column0 = place[0] * PART
-    sigma = width[0]
-    two_var = 2.0 * sigma * sigma
-    norm = gauss_norm(two_var)
-    d_row = lax.broadcasted_iota(jnp.int32, (128, 160), 1) - 16 - lax.broadcasted_iota(jnp.int32, (128, 160), 0)
-    row_hi, row_lo = split_bf16(gauss_at(d_row, two_var, norm))
-    k = lax.broadcasted_iota(jnp.int32, (PART + 128, PART), 0)
-    x = lax.broadcasted_iota(jnp.int32, (PART + 128, PART), 1)
-    source = jnp.where(k < PART, k, jnp.where(k < PART + 16, k - PART - 16, jnp.where(k < PART + 32, k - 16, 4 * COLS)))
-    col_hi, col_lo = split_bf16(gauss_at(source - x, two_var, norm))
-
-    xs = lax.broadcasted_iota(jnp.int32, (1, PART), 1) + column0
-    zero = jnp.zeros((1, PART), F32)
-    depth_cols = zero
-    r = lax.broadcasted_iota(jnp.int32, (PIECE, PART), 0)
-    here = jnp.zeros((PIECE, PART), F32)
-    before = jnp.zeros((PIECE, PART), F32)
-    after = jnp.zeros((PIECE, PART), F32)
-    for m in range(2 * HALF + 1):
-        d = float(m - HALF)
-        tap = jnp.exp(jnp.full((1, PART), -d * d, F32) / two_var) / norm
-        sq = tap * tap
-        at = xs + (m - HALF)
-        depth_cols = depth_cols + jnp.where((at >= 0) & (at < COLS), sq, 0.0)
-        row = r + (m - HALF)
-        before = before + jnp.where(row < 0, sq, 0.0)
-        after = after + jnp.where(row >= PIECE, sq, 0.0)
-        here = here + jnp.where((row >= 0) & (row < PIECE), sq, 0.0)
-
-    def block(n, carry):
-        y = pl.multiple_of(n * 128, 128)
-        window = ext[pl.ds(y, 160), :]
-        across = dot(row_hi, window) + dot(row_lo, window)
-        a_hi, a_lo = split_bf16(across)
-        signal = dot(a_hi, col_hi) + (dot(a_lo, col_hi) + dot(a_hi, col_lo))
-        for h in range(2):
-            s = n * 2 + h
-            c = cover[pl.ds(s + 1, 1), :]
-            depth_rows = cover[pl.ds(s, 1), :] * before + c * here + cover[pl.ds(s + 2, 1), :] * after
-            scale = lax.rsqrt(jnp.maximum(depth_rows * depth_cols, FLOOR))
-            rows = pl.ds(pl.multiple_of(y + h * PIECE, PIECE), PIECE)
-            detection[rows, :] = signal[h * PIECE : (h + 1) * PIECE] * scale
-            own = ext[pl.ds(pl.multiple_of(y + h * PIECE + 16, 16), PIECE), 0:PART].astype(F32)
-            coadd[rows, :] = own / jnp.maximum(c, 1.0)
-        return carry
-
-    lax.fori_loop(0, ROWS // 128, block, 0)
+def detect_kernel(place, width, cover, ext, coadd, detection, rows_band, cols_band, share, depth_cols, across):
+    step = pl.program_id(0)
+
+    @pl.when(step == 0)
+    def _():
+        sigma = width[0]
+        two_var = 2.0 * sigma * sigma
+        norm = gauss_norm(two_var)
+        d_row = lax.broadcasted_iota(jnp.int32, (128, 160), 1) - 16 - lax.broadcasted_iota(jnp.int32, (128, 160), 0)
+        rows_band[0:128, :], rows_band[128:256, :] = split_bf16(gauss_at(d_row, two_var, norm))
+        k = lax.broadcasted_iota(jnp.int32, (PART + 128, PART), 0)
+        x = lax.broadcasted_iota(jnp.int32, (PART + 128, PART), 1)
+        source = jnp.where(
+            k < PART, k, jnp.where(k < PART + 16, k - PART - 16, jnp.where(k < PART + 32, k - 16, 4 * COLS))
+        )
+        cols_band[0], cols_band[1] = split_bf16(gauss_at(source - x, two_var, norm))
+        xs = lax.broadcasted_iota(jnp.int32, (1, PART), 1) + place[0] * PART
+        r = lax.broadcasted_iota(jnp.int32, (PIECE, 128), 0)
+        columns = jnp.zeros((1, PART), F32)
+        before = jnp.zeros((PIECE, 128), F32)
+        after = jnp.zeros((PIECE, 128), F32)
+        inner = jnp.zeros((PIECE, 128), F32)
+        for m in range(2 * HALF + 1):
+            d = float(m - HALF)
+            tap = jnp.exp(jnp.full((1, 128), -d * d, F32) / two_var) / norm
+            sq = tap * tap
+            at = xs + (m - HALF)
+            columns = columns + jnp.where((at >= 0) & (at < COLS), jnp.concatenate([sq, sq], axis=1), 0.0)
+            row = r + (m - HALF)
+            inner = inner + jnp.where((row >= 0) & (row < PIECE), sq, 0.0)
+            if m < HALF:
+                before = before + jnp.where(row < 0, sq, 0.0)
+            if m > HALF:
+                after = after + jnp.where(row >= PIECE, sq, 0.0)
+        depth_cols[...] = columns
+        share[0] = before
+        share[1] = after
+        share[2] = inner
+
+    top = step * DETECT_ROWS
+    for n in range(DETECT_ROWS // 128):
+        window = ext[pl.ds(pl.multiple_of(top + n * 128, 128), 160), :]
+        both = dot(rows_band[...], window)
+        hi, lo = split_bf16(both[0:128] + both[128:256])
+        across[0, n * 128 : (n + 1) * 128, :] = hi
+        across[1, n * 128 : (n + 1) * 128, :] = lo
+    signal = dot(across[0], cols_band[0]) + (dot(across[1], cols_band[0]) + dot(across[0], cols_band[1]))
+    for p in range(DETECT_ROWS // PIECE):
+        s = step * (DETECT_ROWS // PIECE) + p
+        c = cover[pl.ds(s + 1, 1), :]
+        over, under = cover[pl.ds(s, 1), :][:, 0:128], cover[pl.ds(s + 2, 1), :][:, 0:128]
+        depth_rows = over * share[0] + c[:, 0:128] * share[2] + under * share[1]
+        rows = slice(p * PIECE, (p + 1) * PIECE)
+        for l in range(PART // 128):
+            lanes = slice(l * 128, (l + 1) * 128)
+            scale = lax.rsqrt(jnp.maximum(depth_rows * depth_cols[:, lanes], FLOOR))
+            detection[rows, lanes] = signal[rows, lanes] * scale
+        own = ext[pl.ds(pl.multiple_of(top + p * PIECE + 16, 16), PIECE), 0:PART].astype(F32)
+        coadd[rows, :] = own * (1.0 / jnp.maximum(c, 1.0))
 
 
 def detect(place, width, cover, ext):
     smem = pl.BlockSpec(memory_space=pltpu.SMEM)
-    vmem = pl.BlockSpec(memory_space=pltpu.VMEM)
     out = jax.ShapeDtypeStruct((ROWS, PART), F32)
+    block = pl.BlockSpec((DETECT_ROWS, PART), lambda n: (n, 0))
     return pl.pallas_call(
         detect_kernel,
         out_shape=(out, out),
-        in_specs=[smem, smem, vmem, vmem],
+        grid=(ROWS // DETECT_ROWS,),
+        in_specs=[
+            smem,
+            smem,
+            pl.BlockSpec((40, PART), lambda n: (0, 0)),
+            pl.BlockSpec((ROWS + 32, PART + 128), lambda n: (0, 0)),
+        ],
+        out_specs=(block, block),
+        scratch_shapes=[
+            pltpu.VMEM((256, 160), BF16),
+            pltpu.VMEM((2, PART + 128, PART), BF16),
+            pltpu.VMEM((3, PIECE, 128), F32),
+            pltpu.VMEM((1, PART), F32),
+            pltpu.VMEM((2, DETECT_ROWS, PART + 128), BF16),
+        ],
         compiler_params=pltpu.CompilerParams(vmem_limit_bytes=VMEM_LIMIT),
         name="detect",
     )(place, width, cover, ext)

time: 116 us -> 103 us (0.89)
  the two profiles are of different devices: /device:TPU:1 before, /device:TPU:56 now
where the time goes in v4:
time: 103 us
  Pallas kernels  101 us (98%)
  between operations  1.94 us (2%)
    pallas_call x1, Pallas kernels, coadd(): pl.pallas_call(coadd_kernel, out_shape=(jax.ShapeDtypeStruct((ROWS + 32,...  94.6 us
    pallas_call x1, Pallas kernels, detect(): pl.pallas_call(detect_kernel, out_shape=(out, out), grid=(ROWS // DETECT_...  6.07 us

profile of v4, /device:TPU:56, one launch (start us, length us, event | category | flops | bytes accessed | tf_op | source)
XLA Modules:
  0.0 102.6 jit_solution(5369785942308162397)
XLA Ops:
  1.9 94.6 %coadd.1 = (bf16[2080,384]{1,0:T(8,128)(2,1)}, f32[40,256]{1,0:T(8,128)}) custom-call(f32[3]{0:T(128)} %bitcast.10, f32[3]{0:T(128)} %widths.1, s32[1]{0:T(128)S(6)} %copy.12.weight, s32[1,32]{1,0:T(1,128)} %bitcast.11, s32[1,32]{1,0:T(1,128)} %bitcast.12, bf16[2048,1024]{1,0:T(8,128)(2,1)} %bitcast.8, bf16[32,64,2048]{2,1,0:T(8,128)(2,1)} %bitcast.7, ...), custom_call_target="tpu_custom_call" | custom-call | flops 30000001024 | bytes 18874368 | tf_op jit(solution)/shard_map/coadd/pallas_call | solution.py:346
  96.5 6.1 %detect.1 = (f32[2048,256]{1,0:T(8,128)}, f32[2048,256]{1,0:T(8,128)}) custom-call(s32[1]{0:T(128)} %bitcast.place, f32[1]{0:T(128)S(6)} %copy.11.width, f32[40,256]{1,0:T(8,128)} %get-tuple-element.4.cover, bf16[2080,384]{1,0:T(8,128)(2,1)} %get-tuple-element.5.ext), custom_call_target="tpu_custom_call" | custom-call | tf_op jit(solution)/shard_map/detect/pallas_call | solution.py:465

commit v5 on v4

--- a/solution.py
+++ b/solution.py
@@ -67,7 +67,7 @@
 
 
 def partner(here, step, n):
-    m = lax.rem(n * 11, 32)
+    m = lax.rem(n * 21, 32)
     dz = lax.div(m, 8)
     return beyond(here, dz, lax.rem(step + 4 - dz, 4), lax.rem(lax.div(m, 4), 2), lax.rem(m, 4))
 
@@ -126,19 +126,24 @@
     ]
     for c in image_copies + wr_copies[:1] + wc_copies[:4] + wr_copies[1:] + wc_copies[4:]:
         c.start()
-    lax.fori_loop(1, DEVICES, greet, 0)
+    for k in range(1, 8):
+        greet(k, 0)
+    lax.fori_loop(8, DEVICES, greet, 0, unroll=8)
     img[0:16, :] = jnp.zeros((16, COLS), BF16)
     img[ROWS + 16 : ROWS + 32, :] = jnp.zeros((16, COLS), BF16)
     rp[:, :, 0:128] = jnp.zeros((NBASIS, CHUNK, 128), BF16)
     rp[:, :, COLS + 128 : COLS + 256] = jnp.zeros((NBASIS, CHUNK, 128), BF16)
     d_row = lax.broadcasted_iota(jnp.int32, (128, 160), 1) - 16 - lax.broadcasted_iota(jnp.int32, (128, 160), 0)
-    d_col = lax.broadcasted_iota(jnp.int32, (512, 256), 0) - 128 - lax.broadcasted_iota(jnp.int32, (512, 256), 1)
+    d_col = lax.broadcasted_iota(jnp.int32, (160, 128), 0) - 16 - lax.broadcasted_iota(jnp.int32, (160, 128), 1)
+    cb[...] = jnp.zeros((NBASIS, 512, 256), BF16)
     for b in range(NBASIS):
         sigma = widths[b]
         two_var = 2.0 * sigma * sigma
         norm = gauss_norm(two_var)
         rb[b * 128 : (b + 1) * 128, :] = gauss_at(d_row, two_var, norm).astype(BF16)
-        cb[b] = gauss_at(d_col, two_var, norm).astype(BF16)
+        band = gauss_at(d_col, two_var, norm).astype(BF16)
+        cb[b, 112:272, 0:128] = band
+        cb[b, 240:400, 128:256] = band
 
     for n in range(ROWS // CHUNK):
         image_copies[n].wait()

time: 103 us -> 101 us (0.981)
  the two profiles are of different devices: /device:TPU:56 before, /device:TPU:1 now
where the time goes in v5:
time: 101 us
  Pallas kernels  98.6 us (98%)
  between operations  1.94 us (2%)
    pallas_call x1, Pallas kernels, coadd(): pl.pallas_call(coadd_kernel, out_shape=(jax.ShapeDtypeStruct((ROWS + 32,...  92.6 us
    pallas_call x1, Pallas kernels, detect(): pl.pallas_call(detect_kernel, out_shape=(out, out), grid=(ROWS // DETECT_...  6.07 us

profile of v5, /device:TPU:1, one launch (start us, length us, event | category | flops | bytes accessed | tf_op | source)
XLA Modules:
  0.0 100.6 jit_solution(4927013750934295729)
XLA Ops:
  1.9 92.6 %coadd.1 = (bf16[2080,384]{1,0:T(8,128)(2,1)}, f32[40,256]{1,0:T(8,128)}) custom-call(f32[3]{0:T(128)} %bitcast.10, f32[3]{0:T(128)} %widths.1, s32[1]{0:T(128)S(6)} %copy.12.weight, s32[1,32]{1,0:T(1,128)} %bitcast.11, s32[1,32]{1,0:T(1,128)} %bitcast.12, bf16[2048,1024]{1,0:T(8,128)(2,1)} %bitcast.8, bf16[32,64,2048]{2,1,0:T(8,128)(2,1)} %bitcast.7, ...), custom_call_target="tpu_custom_call" | custom-call | flops 30000001024 | bytes 18874368 | tf_op jit(solution)/shard_map/coadd/pallas_call | solution.py:351
  94.5 6.1 %detect.1 = (f32[2048,256]{1,0:T(8,128)}, f32[2048,256]{1,0:T(8,128)}) custom-call(s32[1]{0:T(128)} %bitcast.place, f32[1]{0:T(128)S(6)} %copy.11.width, f32[40,256]{1,0:T(8,128)} %get-tuple-element.4.cover, bf16[2080,384]{1,0:T(8,128)(2,1)} %get-tuple-element.5.ext), custom_call_target="tpu_custom_call" | custom-call | tf_op jit(solution)/shard_map/detect/pallas_call | solution.py:470
